TPU v7x, 256 devices: a whole 4x4x8 slice. The times are simulated.
256 devices in a mesh: leaf: 64 (over y, z, core), sub: 4 (over x).
Axes of the slice: x: 4, y: 4, z: 8, core: 2. Of those that a mesh axis runs over, the one named last changes fastest.
Arguments:
- vectors: bfloat16 [8, 524288], P(None, ('leaf', 'sub')), may hold values from -6 to 6
- basis: bfloat16 [2048, 64, 256], P(('leaf', 'sub')), may hold values from -0.375 to 0.375
- nearfield_dense_blocks: bfloat16 [2048, 256, 768], P(('leaf', 'sub')), may hold values from -0.21875 to 0.21875
- transfer: bfloat16 [2048, 64, 64], P(('leaf', 'sub')), may hold values from -0.125 to 0.125
- far_tree: int32 [2048, 8], P(('leaf', 'sub')), may hold values from 0 to 63, all different within a row; in each aligned block of 8 rows (0 to 7, 8 to 15, ...) at most 2 rows name the same one
- far_offset: int32 [2048, 8], P(('leaf', 'sub')), may hold values from 0 to 31
- far_coupling: bfloat16 [2048, 8, 64, 64], P(('leaf', 'sub')), may hold values from -0.25 to 0.25
- top_source: int32 [64, 8], P('leaf'), may hold values from 0 to 63
- root_coupling_matrix: bfloat16 [64, 8, 64, 64], P('leaf'), may hold values from -0.25 to 0.25
Outputs:
- product: bfloat16 [8, 524288], P(None, ('leaf', 'sub'))
Inputs may be any that keep to these rules, and one draw needn't show every extreme that they name: `far_tree`: the 8 leaves of one device (aligned blocks of rows) name one subtree in at most 2 entries in all, and some subtree in exactly 2; the entries of one row are distinct.
All inputs are finite; a program needn't handle non-finite values.
Results may differ from a plain program's by a relative error of at most 0.0037.
Values may be sent and summed in bfloat16 or wider, within the bound.
A program may use at most 64 MiB of HBM per device.

v0:
```python
import jax
import jax.numpy as jnp
from jax import lax
from jax.sharding import PartitionSpec as P


def extended(array, sides, width):
    for axis, dim in sides:
        peers, length = (lax.axis_size(axis), array.shape[dim])
        up = [(i, (i + 1) % peers) for i in range(peers - 1)]
        down = [(j, i) for i, j in up]
        last = lax.slice_in_dim(array, length - width, length, axis=dim)
        first = lax.slice_in_dim(array, 0, width, axis=dim)
        before = lax.ppermute(last, axis, up)
        after = lax.ppermute(first, axis, down)
        array = jnp.concatenate([before, array, after], axis=dim)
    return array


def shards(
    vectors,
    basis,
    nearfield_dense_blocks,
    transfer,
    far_tree,
    far_offset,
    far_coupling,
    top_source,
    root_coupling_matrix,
):
    vec_count = vectors.shape[0]
    point_count = vectors.shape[1]
    leaf_count = basis.shape[0]
    rank_size = basis.shape[1]
    leaf_width = basis.shape[2]
    link_count = far_tree.shape[1]
    group_size = leaf_count * lax.axis_size("sub")
    leaf_vals = vectors.reshape(vec_count, leaf_count, leaf_width)
    leaf_coef = jnp.einsum(
        "lrp,vlp->lrv", basis, leaf_vals, preferred_element_type=jnp.float32
    ).astype(jnp.bfloat16)
    flat_coef = leaf_coef.reshape(leaf_count, rank_size * vec_count)
    subtree = lax.all_gather(flat_coef, "sub", axis=0, tiled=True)
    everything = lax.all_gather(subtree, "leaf", axis=0, tiled=True)
    source_index = (far_tree * group_size + far_offset).reshape(-1)
    picked = everything[source_index]
    picked = picked.reshape(leaf_count, link_count, rank_size, vec_count)
    far_local = jnp.einsum(
        "lfrs,lfsv->lrv", far_coupling, picked, preferred_element_type=jnp.float32
    )
    partial_sum = jnp.einsum("lrs,lrv->sv", transfer, leaf_coef, preferred_element_type=jnp.float32)
    node_total = lax.psum(partial_sum, "sub")
    node_coef = lax.all_gather(node_total.astype(jnp.bfloat16)[None], "leaf", axis=0, tiled=True)
    selected_entry = node_coef[top_source[0]]
    root_local_expansion = jnp.einsum(
        "frs,fsv->rv", root_coupling_matrix[0], selected_entry, preferred_element_type=jnp.float32
    )
    downward = jnp.einsum(
        "lrs,sv->lrv",
        transfer.astype(jnp.float32),
        root_local_expansion,
        precision=lax.Precision.HIGHEST,
    )
    downward_coefficient = (far_local + downward).astype(jnp.bfloat16)
    far_part = jnp.einsum(
        "lrp,lrv->vlp", basis, downward_coefficient, preferred_element_type=jnp.float32
    )
    padded = extended(vectors, ((("leaf", "sub"), 1),), leaf_width)
    blocks = padded.reshape(vec_count, leaf_count + 2, leaf_width)
    neighbor_span = jnp.concatenate([blocks[:, :-2], blocks[:, 1:-1], blocks[:, 2:]], axis=2)
    nearfield_portion = jnp.einsum(
        "fem,ebm->feb", neighbor_span, nearfield_dense_blocks, preferred_element_type=jnp.float32
    )
    return (nearfield_portion + far_part).reshape(vec_count, point_count).astype(jnp.bfloat16)


def solution(mesh):
    placed = (
        P(None, ("leaf", "sub")),
        P(("leaf", "sub"), None, None),
        P(("leaf", "sub"), None, None),
        P(("leaf", "sub"), None, None),
        P(("leaf", "sub"), None),
        P(("leaf", "sub"), None),
        P(("leaf", "sub"), None, None, None),
        P("leaf", None),
        P("leaf", None, None, None),
    )
    return jax.shard_map(
        shards, mesh=mesh, in_specs=placed, out_specs=P(None, ("leaf", "sub")), check_vma=False
    )
```

profile of v0, /device:TPU:1, one launch (start us, length us, event | category | flops | bytes accessed | tf_op | source)
XLA Modules:
  0.0 119.3 jit_solution(1645211475650218830)
XLA Ops:
  6.5 1.3 %convolution_convert_fusion = bf16[8,64,8]{1,2,0:T(8,128)(2,1)S(1)} fusion(bf16[8,64,256]{2,1,0:T(8,128)(2,1)} %param.10, bf16[8,8,256]{2,0,1:T(8,128)(2,1)} %bitcast.46), kind=kOutput, calls=%fused_computation.8 | convolution fusion | flops 2101248 | bytes 303104 | tf_op jit(solution)/shard_map/lrp,vlp->lrv/dot_general | solution.py:39
  7.8 0.1 copy.11
  8.0 0.2 reshape.75
  8.1 11.1 %all_gather.9 = bf16[32,512]{1,0:T(8,128)(2,1)} all-gather(bf16[8,512]{1,0:T(8,128)(2,1)S(1)} %reshape.75), channel_id=1, replica_groups=mesh['leaf'=64,'sub'=4] {'sub'}, dimensions={0}, use_global_device_ids=true | all-gather | bytes 40960 | tf_op jit(solution)/shard_map/all_gather | solution.py:43
  19.3 0.7 fusion.15
  20.0 2.9 %collective-permute-start = (bf16[8,256]{1,0:T(8,128)(2,1)S(1)}, bf16[8,256]{1,0:T(8,128)(2,1)S(1)}, u32[]{:S(2)}, u32[]{:S(2)}) collective-permute-start(bf16[8,256]{1,0:T(8,128)(2,1)S(1)} %get-tuple-element.8), channel_id=1, source_target_pairs={{0,1},{1,2},{2,3},{3,4},{4,5},{5,6},{6,7},{7,8},{8,9},{9,10},{10,1... | collective-permute-start | bytes 12296 | tf_op jit(solution)/shard_map/ppermute | solution.py:14
  22.8 6.3 %collective-permute-start.1 = (bf16[8,256]{1,0:T(8,128)(2,1)S(1)}, bf16[8,256]{1,0:T(8,128)(2,1)S(1)}, u32[]{:S(2)}, u32[]{:S(2)}) collective-permute-start(bf16[8,256]{1,0:T(8,128)(2,1)S(1)} %get-tuple-element.9), channel_id=1, source_target_pairs={{1,0},{2,1},{3,2},{4,3},{5,4},{6,5},{7,6},{8,7},{9,8},{10,9},{11,1... | collective-permute-start | bytes 12296 | tf_op jit(solution)/shard_map/ppermute | solution.py:15
  29.2 0.7 multiply_add_fusion
  29.9 0.1 reshape.76
  30.0 1.1 convolution_bitcast_fusion.2
  31.1 7.9 %psum.7 = bf16[64,8]{0,1:T(8,128)(2,1)S(1)} all-reduce(f32[64,8]{0,1:T(8,128)S(1)} %convolution_bitcast_fusion.2), channel_id=1, replica_groups=mesh['leaf'=64,'sub'=4] {'sub'}, use_global_device_ids=true, to_apply=%region_0.0 | all-reduce | flops 512 | bytes 3072 | tf_op jit(solution)/shard_map/psum | solution.py:52
  39.0 55.0 %all-gather.1 = bf16[64,64,8]{1,2,0:T(8,128)(2,1)S(1)} all-gather(bf16[1,64,8]{1,2,0:T(8,128)(2,1)S(1)} %bitcast.47), channel_id=2, replica_groups=mesh['leaf'=64,'sub'=4] {'leaf'}, dimensions={0}, use_global_device_ids=true | all-gather | bytes 66560 | tf_op jit(solution)/shard_map/all_gather | solution.py:53
  94.0 0.7 fusion.12
  94.7 0.6 gather_fusion.1
  95.3 1.0 fusion.3
  96.3 0.0 collective-permute-done
  96.3 0.8 pad_maximum_fusion
  97.1 1.5 %fusion.5 = f32[8,8,256]{2,1,0:T(8,128)} fusion(bf16[8,256,768]{2,1,0:T(8,128)(2,1)S(1)} %copy-done, bf16[8,8,256]{2,0,1:T(8,128)(2,1)S(1)} %get-tuple-element.6, bf16[8,8,256]{2,0,1:T(8,128)(2,1)S(1)} %get-tuple-element.7, bf16[8,8,256]{2,0,1:T(8,128)(2,1)S(1)} %get-tuple-element.5), kind=kOutput, calls=%fused_computation.12 | convolution fusion | flops 25460736 | bytes 3309568 | tf_op jit(solution)/shard_map/fem,ebm->feb/dot_general | solution.py:71
  98.7 3.5 %all-gather.4.cloned.1.call-done = bf16[2048,512]{1,0:T(8,128)(2,1)} async-done(((bf16[32,512]{1,0:T(8,128)(2,1)}), bf16[2048,512]{1,0:T(8,128)(2,1)}) %all-gather.4.cloned.1.call-update) | async-done | bytes 2097168 | tf_op jit(solution)/shard_map/all_gather | solution.py:44
  102.2 3.2 %gather_fusion = bf16[64,512]{1,0:T(8,128)(2,1)} fusion(bf16[2048,512]{1,0:T(8,128)(2,1)} %all-gather.4.cloned.1.call-done, s32[1024]{0:T(1024)S(1)} %pad_clamp_fusion.1), kind=kCustom, calls=%fused_computation | custom fusion | bytes 131328 | tf_op jit(solution)/shard_map/gather | solution.py:46
  105.4 3.0 %reshape.77 = bf16[8,8,64,8]{3,2,1,0:T(8,128)(2,1)} reshape(bf16[64,512]{1,0:T(8,128)(2,1)} %gather_fusion) | data formatting | bytes 131072 | tf_op jit(solution)/shard_map/reshape | solution.py:47
  108.4 2.0 %convolution_bitcast_fusion.1 = f32[8,64,8]{1,2,0:T(8,128)S(1)} fusion(bf16[8,8,64,8]{3,2,1,0:T(8,128)(2,1)} %reshape.77, bf16[8,8,64,64]{3,2,1,0:T(8,128)(2,1)} %param.15), kind=kOutput, calls=%fused_computation.6 | convolution fusion | flops 4194304 | bytes 606208 | tf_op jit(solution)/shard_map/lfrs,lfsv->lrv/dot_general | solution.py:48
  110.4 0.4 fusion.2
  110.8 1.6 %fusion = bf16[8,8,256]{2,1,0:T(8,128)(2,1)} fusion(f32[8,8,256]{2,1,0:T(8,128)} %fusion.5, bf16[8,64,8]{1,2,0:T(8,128)(2,1)S(1)} %fusion.2, bf16[8,64,256]{2,1,0:T(8,128)(2,1)S(1)} %copy-done.1), kind=kOutput, calls=%fused_computation.3 | convolution fusion | flops 2129920 | bytes 368640 | tf_op jit(solution)/shard_map/lrp,lrv->vlp/dot_general | solution.py:65
  (13 shorter events, 0.1 us)
Async XLA Ops:
  6.5 90.6 %copy-start = (bf16[8,256,768]{2,1,0:T(8,128)(2,1)S(1)}, bf16[8,256,768]{2,1,0:T(8,128)(2,1)}, u32[]{:S(2)}) copy-start(bf16[8,256,768]{2,1,0:T(8,128)(2,1)} %param.11) | copy-start | bytes 9437188
  6.5 95.6 %all-gather.4.cloned.1.call-start = ((), (), s32[]{:S(2)}) async-start(), calls=%async_computation | async-start | bytes 2129920 | tf_op jit(solution)/shard_map/all_gather | solution.py:44
  20.0 76.3 %collective-permute-start = (bf16[8,256]{1,0:T(8,128)(2,1)S(1)}, bf16[8,256]{1,0:T(8,128)(2,1)S(1)}, u32[]{:S(2)}, u32[]{:S(2)}) collective-permute-start(bf16[8,256]{1,0:T(8,128)(2,1)S(1)} %get-tuple-element.8), channel_id=1, source_target_pairs={{0,1},{1,2},{2,3},{3,4},{4,5},{5,6},{6,7},{7,8},{8,9},{9,10},{10,1... | collective-permute-start | bytes 12296 | tf_op jit(solution)/shard_map/ppermute | solution.py:14
  22.8 73.5 %collective-permute-start.1 = (bf16[8,256]{1,0:T(8,128)(2,1)S(1)}, bf16[8,256]{1,0:T(8,128)(2,1)S(1)}, u32[]{:S(2)}, u32[]{:S(2)}) collective-permute-start(bf16[8,256]{1,0:T(8,128)(2,1)S(1)} %get-tuple-element.9), channel_id=1, source_target_pairs={{1,0},{2,1},{3,2},{4,3},{5,4},{6,5},{7,6},{8,7},{9,8},{10,9},{11,1... | collective-permute-start | bytes 12296 | tf_op jit(solution)/shard_map/ppermute | solution.py:15
  97.1 13.3 %copy-start.2 = (bf16[8,64,64]{2,1,0:T(8,128)(2,1)S(1)}, bf16[8,64,64]{2,1,0:T(8,128)(2,1)}, u32[]{:S(2)}) copy-start(bf16[8,64,64]{2,1,0:T(8,128)(2,1)} %param.12) | copy-start | bytes 196612
  97.1 13.7 %copy-start.1 = (bf16[8,64,256]{2,1,0:T(8,128)(2,1)S(1)}, bf16[8,64,256]{2,1,0:T(8,128)(2,1)}, u32[]{:S(2)}) copy-start(bf16[8,64,256]{2,1,0:T(8,128)(2,1)} %param.10) | copy-start | bytes 786436
Sparse Core Ops, SparseCore 0:
  19.4 82.7 all-gather.3
where the time goes:
time: 120 us; the launch traced here: 119 us
  blocking collectives  74 us (62%)
  between operations  13.5 us (11%)
  starting transfers between devices  9.18 us (8%)
  matrix products  8.98 us (7%)
  local copies, waits for them, and re-layouts  7.95 us (7%)
  waiting for transfers between devices  3.54 us (3%)
  other arithmetic  2.15 us (2%)
    all_gather x1, blocking collectives, shards(): lax.all_gather(node_total.astype(jnp.bfloat16)[None], 'leaf', axis=0, til...  55 us
    all_gather x1, blocking collectives, shards(): subtree = lax.all_gather(flat_coef, 'sub', axis=0, tiled=True)  11.1 us
    psum x1, blocking collectives, shards(): node_total = lax.psum(partial_sum, 'sub')  7.92 us
    ppermute x1, starting transfers between devices, extended(): after = lax.ppermute(first, axis, down)  6.32 us
    all_gather x1, waiting for transfers between devices, shards(): everything = lax.all_gather(subtree, 'leaf', axis=0, tiled=True)  3.5 us
    gather x1, local copies, waits for them, and re-layouts, shards(): picked = everything[source_index]  3.19 us
    reshape x1, local copies, waits for them, and re-layouts, shards(): picked = picked.reshape(leaf_count, link_count, rank_size, vec_count)  3.05 us
    ppermute x1, starting transfers between devices, extended(): before = lax.ppermute(last, axis, up)  2.86 us
  transfers between devices with their start and end apart: 3, of which 1 were waited for; matrix products, arithmetic and copies ran while one was open for 6% of the time, Pallas kernels for 0%

commit v1 on v0

v1 whole, which is shorter than its diff:
```python
import functools

import jax
import jax.numpy as jnp
from jax import lax
from jax.experimental import pallas as pl
from jax.experimental.pallas import tpu as pltpu
from jax.sharding import PartitionSpec as P

MESH = pl.DeviceIdType.MESH
F32 = jnp.float32
BF16 = jnp.bfloat16
NT = (((1,), (1,)), ((), ()))
TREES = 64
SUBS = 4
LEAVES = 8
LINKS = 8
NVEC = 8
RANK = 64
WIDTH = 256


def dot(a, b):
    return jnp.dot(a, b, preferred_element_type=F32)


def dot_nt(a, b):
    return lax.dot_general(a, b, NT, preferred_element_type=F32)


def iota(shape, dim):
    return lax.broadcasted_iota(jnp.int32, shape, dim)


def drain(ref, sem):
    pltpu.make_async_copy(ref, ref, sem).wait()


def kernel(
    vec_hbm, basis_hbm, near_hbm, trans_hbm, tree_hbm, offset_hbm, far_hbm, top_hbm, root_hbm,
    out_ref,
    x_v, basis_v, near_v, trans_v, tree_v, offset_v, far_v, root_v, tree_s, top_s,
    prev_v, next_v, table_send, table_recv, coef_send, coef_recv, node_send, node_recv,
    reply_send, reply_recv, picked_v, rank_v, pairs_v, down_v, local_v,
    sem_x, sem_basis, sem_near, sem_trans, sem_table, sem_far, sem_root, sem_smem,
    halo_send, halo_recv, table_ssem, table_rsem, coef_ssem, coef_rsem,
    node_ssem, node_rsem, reply_ssem, reply_rsem,
):
    me = lax.axis_index("leaf")
    sub = lax.axis_index("sub")
    flat = me * SUBS + sub
    after = lax.rem(flat + 1, TREES * SUBS)
    before = lax.rem(flat + TREES * SUBS - 1, TREES * SUBS)
    after_id = {"leaf": after // SUBS, "sub": lax.rem(after, SUBS)}
    before_id = {"leaf": before // SUBS, "sub": lax.rem(before, SUBS)}

    barrier = pltpu.get_barrier_semaphore()

    def greet(i, carry):
        pl.semaphore_signal(
            barrier, inc=1, device_id={"leaf": lax.rem(me + i, TREES)}, device_id_type=MESH
        )
        return carry

    for i in range(1, SUBS):
        pl.semaphore_signal(
            barrier, inc=1, device_id={"sub": lax.rem(sub + i, SUBS)}, device_id_type=MESH
        )
    pl.semaphore_signal(barrier, inc=1, device_id=after_id, device_id_type=MESH)
    pl.semaphore_signal(barrier, inc=1, device_id=before_id, device_id_type=MESH)
    lax.fori_loop(1, TREES, greet, 0)

    get_tree = pltpu.make_async_copy(tree_hbm, tree_v, sem_table.at[0])
    get_offset = pltpu.make_async_copy(offset_hbm, offset_v, sem_table.at[1])
    get_x = pltpu.make_async_copy(vec_hbm, x_v, sem_x)
    get_basis = pltpu.make_async_copy(basis_hbm, basis_v, sem_basis)
    get_trans = pltpu.make_async_copy(trans_hbm, trans_v, sem_trans)
    get_tree_s = pltpu.make_async_copy(tree_hbm, tree_s, sem_smem.at[0])
    get_top_s = pltpu.make_async_copy(top_hbm, top_s, sem_smem.at[1])
    get_far = pltpu.make_async_copy(far_hbm, far_v, sem_far)
    get_root = pltpu.make_async_copy(root_hbm, root_v, sem_root)
    get_near = [
        pltpu.make_async_copy(near_hbm.at[l], near_v.at[l], sem_near.at[l]) for l in range(LEAVES)
    ]
    for copy in (get_x, get_basis, get_tree, get_offset, get_trans, get_tree_s, get_top_s):
        copy.start()
    get_far.start()
    get_root.start()
    for copy in get_near:
        copy.start()

    get_tree.wait()
    get_offset.wait()
    tree = tree_v[...].astype(F32).astype(BF16)
    offset = offset_v[...].astype(F32).astype(BF16)
    lane = iota((LINKS, 128), 1)
    column = iota((LINKS, 128), 0)
    spread = lax.rem(lane, LINKS) == column
    low = jnp.where(spread & (lane < 64), 1.0, 0.0).astype(BF16)
    high = jnp.where(spread & (lane >= 64), 1.0, 0.0).astype(BF16)
    rows = dot(tree, low) + dot(offset, high)
    own_row = lax.rem(lane, 64) // LINKS == column
    table_row = jnp.sum(jnp.where(own_row, rows, 0.0), axis=0, keepdims=True)
    table_send[...] = table_row
    table_recv[pl.ds(me, 1)] = table_row[None]

    get_x.wait()
    get_basis.wait()
    coefs = []
    for l in range(LEAVES):
        c = dot_nt(x_v[:, l * WIDTH : (l + 1) * WIDTH], basis_v[l]).astype(BF16)
        coefs.append(c)
        wide = c.astype(F32)
        wide = jnp.concatenate([wide, wide], axis=1)
        coef_send[0:NVEC, l, :] = wide
    get_trans.wait()
    partial = dot(coefs[0], trans_v[0])
    for l in range(1, LEAVES):
        partial = partial + dot(coefs[l], trans_v[l])
    coef_send[NVEC] = jnp.concatenate([partial, partial], axis=1)

    pl.semaphore_wait(barrier, TREES - 1 + SUBS - 1 + 2)

    for i in range(1, SUBS):
        pltpu.make_async_remote_copy(
            src_ref=coef_send, dst_ref=coef_recv.at[sub], send_sem=coef_ssem, recv_sem=coef_rsem,
            device_id={"sub": lax.rem(sub + i, SUBS)}, device_id_type=MESH,
        ).start()
    to_after = pltpu.make_async_remote_copy(
        src_ref=vec_hbm.at[:, pl.ds((LEAVES - 1) * WIDTH, WIDTH)], dst_ref=prev_v,
        send_sem=halo_send.at[0], recv_sem=halo_recv.at[0], device_id=after_id, device_id_type=MESH,
    )
    to_before = pltpu.make_async_remote_copy(
        src_ref=vec_hbm.at[:, pl.ds(0, WIDTH)], dst_ref=next_v,
        send_sem=halo_send.at[1], recv_sem=halo_recv.at[1], device_id=before_id, device_id_type=MESH,
    )

    def ask(i, carry):
        peer = lax.rem(me + i, TREES)
        pltpu.make_async_remote_copy(
            src_ref=table_send, dst_ref=table_recv.at[me], send_sem=table_ssem, recv_sem=table_rsem,
            device_id={"leaf": peer}, device_id_type=MESH,
        ).start()
        return carry

    lax.fori_loop(1, TREES, ask, 0)
    to_after.start()
    to_before.start()
    coef_recv[pl.ds(sub, 1)] = coef_send[...][None]

    entry = iota((64, LINKS), 0)
    link = iota((64, LINKS), 1)
    pick_row = jnp.where(entry // LINKS == link, 1.0, 0.0).astype(BF16)
    by_entry = dot(pick_row, tree)
    tree_col = jnp.sum(
        jnp.where(lax.rem(entry, LINKS) == link, by_entry, 0.0), axis=1, keepdims=True
    )
    same = (tree_col == table_row[:, 0:64]) & (iota((64, 64), 1) < iota((64, 64), 0))
    rank_col = jnp.sum(jnp.where(same, 1.0, 0.0), axis=1, keepdims=True)
    rank_v[...] = jnp.broadcast_to(rank_col, (64, 128))

    get_far.wait()
    for l in range(LEAVES):
        for f in range(0, LINKS, 2):
            pairs_v[l, :, f * RANK : (f + 2) * RANK] = jnp.concatenate(
                [far_v[l, f], far_v[l, f + 1]], axis=1
            )

    drain(coef_recv.at[pl.ds(0, SUBS - 1)], coef_rsem)
    node = coef_recv[0, NVEC]
    for i in range(1, SUBS):
        node = node + coef_recv[i, NVEC]
    node = node.astype(BF16).astype(F32)
    left = iota((NVEC // 2, 128), 1) < 64
    node_row = jnp.where(left, node[0 : NVEC // 2], node[NVEC // 2 :]).astype(BF16)
    node_send[...] = node_row
    node_recv[pl.ds(me, 1)] = node_row[None]

    def spread_node(i, carry):
        peer = lax.rem(me + i, TREES)
        pltpu.make_async_remote_copy(
            src_ref=node_send, dst_ref=node_recv.at[me], send_sem=node_ssem, recv_sem=node_rsem,
            device_id={"leaf": peer}, device_id_type=MESH,
        ).start()
        return carry

    lax.fori_loop(1, TREES, spread_node, 0)

    drain(table_recv.at[pl.ds(0, TREES - 1)], table_rsem)
    table = table_recv[:, 0, :]
    asked = table[:, 0:64] == me.astype(F32)
    earlier = jnp.where(iota((64, 64), 0) < iota((64, 64), 1), 1.0, 0.0).astype(BF16)
    order = dot(jnp.where(asked, 1.0, 0.0).astype(BF16), earlier)
    named = jnp.where(asked, table[:, 64:128] + 1.0, 0.0)
    first = jnp.sum(jnp.where(order == 0.0, named, 0.0), axis=1, keepdims=True)
    second = jnp.sum(jnp.where(order == 1.0, named, 0.0), axis=1, keepdims=True)
    leaf_no = (iota((64, 32), 1) + 1).astype(F32)
    onehot = jnp.concatenate(
        [jnp.where(first == leaf_no, 1.0, 0.0), jnp.where(second == leaf_no, 1.0, 0.0)], axis=0
    ).astype(BF16)
    left = iota((64, 128), 1) < 64
    for v in range(NVEC):
        source = coef_recv[:, v].reshape(SUBS * LEAVES, 128).astype(BF16)
        both = dot(onehot, source)
        picked_v[:, v, :] = jnp.where(left, both[0:64], both[64:128])
    reply_send[...] = picked_v[...].astype(BF16)
    reply_recv[pl.ds(me, 1)] = reply_send[pl.ds(me, 1)]

    def reply(i, carry):
        peer = lax.rem(me + i, TREES)
        pltpu.make_async_remote_copy(
            src_ref=reply_send.at[peer], dst_ref=reply_recv.at[me],
            send_sem=reply_ssem, recv_sem=reply_rsem,
            device_id={"leaf": peer}, device_id_type=MESH,
        ).start()
        return carry

    lax.fori_loop(1, TREES, reply, 0)

    to_after.wait_recv()
    to_before.wait_recv()
    zero = jnp.zeros((NVEC, WIDTH), BF16)
    front = jnp.where(flat == 0, zero, prev_v[...])
    back = jnp.where(flat == TREES * SUBS - 1, zero, next_v[...])
    for l in range(LEAVES):
        get_near[l].wait()
        parts = [
            front if l == 0 else x_v[:, (l - 1) * WIDTH : l * WIDTH],
            x_v[:, l * WIDTH : (l + 1) * WIDTH],
            back if l == LEAVES - 1 else x_v[:, (l + 1) * WIDTH : (l + 2) * WIDTH],
        ]
        local_v[:, l * WIDTH : (l + 1) * WIDTH] = dot_nt(
            jnp.concatenate(parts, axis=1), near_v[l]
        )

    get_root.wait()
    get_top_s.wait()
    drain(node_recv.at[pl.ds(0, TREES - 1)], node_rsem)
    root_local = None
    for f in range(LINKS):
        n = node_recv[top_s[0, f]].astype(F32)
        n = jnp.concatenate([n[:, 0:64], n[:, 64:128]], axis=0).astype(BF16)
        term = dot_nt(n, root_v[0, f])
        root_local = term if root_local is None else root_local + term
    hi = root_local.astype(BF16)
    rest = root_local - hi.astype(F32)
    mid = rest.astype(BF16)
    lo = (rest - mid.astype(F32)).astype(BF16)
    for l in range(LEAVES):
        down_v[l] = (
            dot_nt(hi, trans_v[l]) + dot_nt(mid, trans_v[l]) + dot_nt(lo, trans_v[l])
        )

    get_tree_s.wait()
    drain(reply_recv.at[pl.ds(0, TREES - 1)], reply_rsem)
    left = iota((NVEC, 128), 1) < 64
    for l in range(LEAVES):
        parts = []
        for f in range(0, LINKS, 2):
            halves = []
            for j in range(2):
                e = l * LINKS + f + j
                got = reply_recv[tree_s[l, f + j]].astype(F32)
                there = jnp.broadcast_to(rank_v[e : e + 1, :], (NVEC, 128)) == float(j)
                halves.append(jnp.where(there, got, pltpu.roll(got, 64, 1)))
            parts.append(jnp.where(left, halves[0], halves[1]))
        coef = jnp.concatenate(parts, axis=1).astype(BF16)
        down = (dot_nt(coef, pairs_v[l]) + down_v[l]).astype(BF16)
        out_ref[:, l * WIDTH : (l + 1) * WIDTH] = (
            local_v[:, l * WIDTH : (l + 1) * WIDTH] + dot(down, basis_v[l])
        ).astype(BF16)

    to_after.wait_send()
    to_before.wait_send()
    drain(coef_recv.at[pl.ds(0, SUBS - 1)], coef_ssem)
    drain(table_recv.at[pl.ds(0, TREES - 1)], table_ssem)
    drain(node_recv.at[pl.ds(0, TREES - 1)], node_ssem)
    drain(reply_recv.at[pl.ds(0, TREES - 1)], reply_ssem)


def shards(vectors, basis, near, transfer, tree, offset, far, top, root):
    dma = pltpu.SemaphoreType.DMA
    scratch = [
        pltpu.VMEM((NVEC, LEAVES * WIDTH), BF16),
        pltpu.VMEM((LEAVES, RANK, WIDTH), BF16),
        pltpu.VMEM((LEAVES, WIDTH, 3 * WIDTH), BF16),
        pltpu.VMEM((LEAVES, RANK, RANK), BF16),
        pltpu.VMEM((LEAVES, LINKS), jnp.int32),
        pltpu.VMEM((LEAVES, LINKS), jnp.int32),
        pltpu.VMEM((LEAVES, LINKS, RANK, RANK), BF16),
        pltpu.VMEM((1, LINKS, RANK, RANK), BF16),
        pltpu.SMEM((LEAVES, LINKS), jnp.int32),
        pltpu.SMEM((1, LINKS), jnp.int32),
        pltpu.VMEM((NVEC, WIDTH), BF16),
        pltpu.VMEM((NVEC, WIDTH), BF16),
        pltpu.VMEM((1, 128), F32),
        pltpu.VMEM((TREES, 1, 128), F32),
        pltpu.VMEM((NVEC + 1, LEAVES, 128), F32),
        pltpu.VMEM((SUBS, NVEC + 1, LEAVES, 128), F32),
        pltpu.VMEM((NVEC // 2, 128), BF16),
        pltpu.VMEM((TREES, NVEC // 2, 128), BF16),
        pltpu.VMEM((TREES, NVEC, 128), BF16),
        pltpu.VMEM((TREES, NVEC, 128), BF16),
        pltpu.VMEM((TREES, NVEC, 128), F32),
        pltpu.VMEM((64, 128), F32),
        pltpu.VMEM((LEAVES, RANK, LINKS * RANK), BF16),
        pltpu.VMEM((LEAVES, NVEC, RANK), F32),
        pltpu.VMEM((NVEC, LEAVES * WIDTH), F32),
        dma,
        dma,
        dma((LEAVES,)),
        dma,
        dma((2,)),
        dma,
        dma,
        dma((2,)),
        dma((2,)),
        dma((2,)),
        dma,
        dma,
        dma,
        dma,
        dma,
        dma,
        dma,
        dma,
    ]
    return pl.pallas_call(
        kernel,
        out_shape=jax.ShapeDtypeStruct(vectors.shape, BF16),
        in_specs=[pl.BlockSpec(memory_space=pl.ANY)] * 9,
        out_specs=pl.BlockSpec(memory_space=pltpu.VMEM),
        scratch_shapes=scratch,
        compiler_params=pltpu.CompilerParams(
            collective_id=0, has_side_effects=True, vmem_limit_bytes=32 * 2**20
        ),
        name="product",
    )(vectors, basis, near, transfer, tree, offset, far, top, root)


def solution(mesh):
    placed = (
        P(None, ("leaf", "sub")),
        P(("leaf", "sub"), None, None),
        P(("leaf", "sub"), None, None),
        P(("leaf", "sub"), None, None),
        P(("leaf", "sub"), None),
        P(("leaf", "sub"), None),
        P(("leaf", "sub"), None, None, None),
        P("leaf", None),
        P("leaf", None, None, None),
    )
    return jax.shard_map(
        shards, mesh=mesh, in_specs=placed, out_specs=P(None, ("leaf", "sub")), check_vma=False
    )
```

time: 120 us -> 35.7 us (0.30)
  blocking collectives: 74 us -> 0 us
  Pallas kernels: 0 us -> 26.1 us
  between operations: 13.5 us -> 0.02 us
  starting transfers between devices: 9.18 us -> 0 us
  matrix products: 8.98 us -> 0 us
  waiting for transfers between devices: 3.54 us -> 0 us
  other arithmetic: 2.15 us -> 0 us
  local copies, waits for them, and re-layouts: 7.95 us -> 9.27 us
    all_gather x2 -> x0, blocking collectives: 66.1 us -> none  [the longest x1 55 us: shards(): lax.all_gather(node_total.astype(jnp.bfloat16)[None], 'leaf', axis=0, til...]
    pallas_call x0 -> x1, Pallas kernels: none -> 26.1 us  [shards(): pl.pallas_call(kernel, out_shape=jax.ShapeDtypeStruct(vectors.shape, BF16...]
    unnamed x6 -> x19, local copies, waits for them, and re-layouts: 0.02 us -> 9.27 us
    ppermute x2 -> x0, starting transfers between devices: 9.18 us -> none  [the longest x1 6.32 us: extended(): after = lax.ppermute(first, axis, down)]
    dot_general x7 -> x0, matrix products: 8.98 us -> none  [the longest x1 1.98 us: shards(): jnp.einsum('lfrs,lfsv->lrv', far_coupling, picked, preferred_element_type...]
    psum x1 -> x0, blocking collectives: 7.92 us -> none  [shards(): node_total = lax.psum(partial_sum, 'sub')]
    gather x2 -> x0, local copies, waits for them, and re-layouts: 3.75 us -> none  [the longest x1 3.19 us: shards(): picked = everything[source_index]]
    all_gather x1 -> x0, waiting for transfers between devices: 3.5 us -> none  [shards(): everything = lax.all_gather(subtree, 'leaf', axis=0, tiled=True)]
  transfers between devices with their start and end apart: 3 -> 0, of which waited for: 1 -> 0; matrix products, arithmetic and copies ran while one was open for 6% -> 0% of each run, Pallas kernels for 0% -> 0%
where the time goes in v1:
time: 35.7 us; the launch traced here: 35.4 us
  Pallas kernels  26.1 us (73%)
  local copies, waits for them, and re-layouts  9.27 us (26%)
    pallas_call x1, Pallas kernels, shards(): pl.pallas_call(kernel, out_shape=jax.ShapeDtypeStruct(vectors.shape, BF16...  26.1 us
    unnamed x19, local copies, waits for them, and re-layouts  9.27 us

profile of v1, /device:TPU:1, one launch (start us, length us, event | category | flops | bytes accessed | tf_op | source)
XLA Modules:
  0.0 35.4 jit_solution(5923945596540518123)
XLA Ops:
  0.0 0.0 copy-start
  0.0 1.9 %copy-done = bf16[8,256,768]{2,1,0:T(8,128)(2,1)S(1)} copy-done((bf16[8,256,768]{2,1,0:T(8,128)(2,1)S(1)}, bf16[8,256,768]{2,1,0:T(8,128)(2,1)}, u32[]{:S(2)}) %copy-start) | copy-done | bytes 3145752
  1.9 0.0 copy-start.1
  1.9 1.2 %copy-done.1 = bf16[8,8,64,64]{3,2,1,0:T(8,128)(2,1)S(1)} copy-done((bf16[8,8,64,64]{3,2,1,0:T(8,128)(2,1)S(1)}, bf16[8,8,64,64]{3,2,1,0:T(8,128)(2,1)}, u32[]{:S(2)}) %copy-start.1) | copy-done | bytes 524312
  3.1 0.0 copy-start.2
  3.1 0.9 %copy-done.2 = bf16[8,64,256]{2,1,0:T(8,128)(2,1)S(1)} copy-done((bf16[8,64,256]{2,1,0:T(8,128)(2,1)S(1)}, bf16[8,64,256]{2,1,0:T(8,128)(2,1)}, u32[]{:S(2)}) %copy-start.2) | copy-done | bytes 262168
  4.1 0.0 copy-start.3
  4.1 0.9 %copy-done.3 = bf16[8,64,64]{2,1,0:T(8,128)(2,1)S(1)} copy-done((bf16[8,64,64]{2,1,0:T(8,128)(2,1)S(1)}, bf16[8,64,64]{2,1,0:T(8,128)(2,1)}, u32[]{:S(2)}) %copy-start.3) | copy-done | bytes 65560
  5.0 0.0 copy-start.4
  5.0 0.9 %copy-done.4 = bf16[1,8,64,64]{3,2,1,0:T(8,128)(2,1)S(1)} copy-done((bf16[1,8,64,64]{3,2,1,0:T(8,128)(2,1)S(1)}, bf16[1,8,64,64]{3,2,1,0:T(8,128)(2,1)}, u32[]{:S(2)}) %copy-start.4) | copy-done | bytes 65560
  5.9 0.0 copy-start.5
  5.9 0.8 %copy-done.5 = bf16[8,2048]{1,0:T(8,128)(2,1)S(1)} copy-done((bf16[8,2048]{1,0:T(8,128)(2,1)S(1)}, bf16[8,2048]{1,0:T(8,128)(2,1)}, u32[]{:S(2)}) %copy-start.5) | copy-done | bytes 32792
  6.6 0.0 copy-start.6
  6.6 0.7 %copy-done.6 = s32[8,8]{1,0:T(8,128)S(1)} copy-done((s32[8,8]{1,0:T(8,128)S(1)}, s32[8,8]{1,0:T(8,128)}, u32[]{:S(2)}) %copy-start.6) | copy-done | bytes 280
  7.3 0.0 copy-start.7
  7.3 0.7 %copy-done.7 = s32[8,8]{1,0:T(8,128)S(1)} copy-done((s32[8,8]{1,0:T(8,128)S(1)}, s32[8,8]{1,0:T(8,128)}, u32[]{:S(2)}) %copy-start.7) | copy-done | bytes 280
  8.0 0.0 copy-start.8
  8.0 0.7 %copy-done.8 = s32[1,8]{1,0:T(1,128)S(1)} copy-done((s32[1,8]{1,0:T(1,128)S(1)}, s32[1,8]{1,0:T(1,128)}, u32[]{:S(2)}) %copy-start.8) | copy-done | bytes 56
  8.7 26.1 %product.1 = bf16[8,2048]{1,0:T(8,128)(2,1)S(1)} custom-call(bf16[8,2048]{1,0:T(8,128)(2,1)S(1)} %copy-done.5, bf16[8,64,256]{2,1,0:T(8,128)(2,1)S(1)} %copy-done.2, bf16[8,256,768]{2,1,0:T(8,128)(2,1)S(1)} %copy-done, bf16[8,64,64]{2,1,0:T(8,128)(2,1)S(1)} %copy-done.3, s32[8,8]{1,0:T(8,128)S(1)} %copy-done.6, s32[8,8]{1,0:T(8,128)S(1)} %copy-done.7, ...), custom_call_target="tpu_custom_call" | custom-call | tf_op jit(solution)/shard_map/product/pallas_call | solution.py:328
  34.7 0.6 %copy.11 = bf16[8,2048]{1,0:T(8,128)(2,1)} copy(bf16[8,2048]{1,0:T(8,128)(2,1)S(1)} %product.1) | data formatting | bytes 65536
Async XLA Ops:
  0.0 1.9 %copy-start = (bf16[8,256,768]{2,1,0:T(8,128)(2,1)S(1)}, bf16[8,256,768]{2,1,0:T(8,128)(2,1)}, u32[]{:S(2)}) copy-start(bf16[8,256,768]{2,1,0:T(8,128)(2,1)} %near_hbm.1) | copy-start | bytes 9437188
  1.9 1.2 %copy-start.1 = (bf16[8,8,64,64]{3,2,1,0:T(8,128)(2,1)S(1)}, bf16[8,8,64,64]{3,2,1,0:T(8,128)(2,1)}, u32[]{:S(2)}) copy-start(bf16[8,8,64,64]{3,2,1,0:T(8,128)(2,1)} %far_hbm.1) | copy-start | bytes 1572868
  3.1 0.9 %copy-start.2 = (bf16[8,64,256]{2,1,0:T(8,128)(2,1)S(1)}, bf16[8,64,256]{2,1,0:T(8,128)(2,1)}, u32[]{:S(2)}) copy-start(bf16[8,64,256]{2,1,0:T(8,128)(2,1)} %basis_hbm.1) | copy-start | bytes 786436
  4.1 0.9 %copy-start.3 = (bf16[8,64,64]{2,1,0:T(8,128)(2,1)S(1)}, bf16[8,64,64]{2,1,0:T(8,128)(2,1)}, u32[]{:S(2)}) copy-start(bf16[8,64,64]{2,1,0:T(8,128)(2,1)} %trans_hbm.1) | copy-start | bytes 196612
  5.0 0.9 %copy-start.4 = (bf16[1,8,64,64]{3,2,1,0:T(8,128)(2,1)S(1)}, bf16[1,8,64,64]{3,2,1,0:T(8,128)(2,1)}, u32[]{:S(2)}) copy-start(bf16[1,8,64,64]{3,2,1,0:T(8,128)(2,1)} %root_hbm.1) | copy-start | bytes 196612
  5.9 0.8 %copy-start.5 = (bf16[8,2048]{1,0:T(8,128)(2,1)S(1)}, bf16[8,2048]{1,0:T(8,128)(2,1)}, u32[]{:S(2)}) copy-start(bf16[8,2048]{1,0:T(8,128)(2,1)} %vec_hbm.1) | copy-start | bytes 98308
  6.6 0.7 %copy-start.6 = (s32[8,8]{1,0:T(8,128)S(1)}, s32[8,8]{1,0:T(8,128)}, u32[]{:S(2)}) copy-start(s32[8,8]{1,0:T(8,128)} %tree_hbm.1) | copy-start | bytes 772
  7.3 0.7 %copy-start.7 = (s32[8,8]{1,0:T(8,128)S(1)}, s32[8,8]{1,0:T(8,128)}, u32[]{:S(2)}) copy-start(s32[8,8]{1,0:T(8,128)} %offset_hbm.1) | copy-start | bytes 772
  8.0 0.7 %copy-start.8 = (s32[1,8]{1,0:T(1,128)S(1)}, s32[1,8]{1,0:T(1,128)}, u32[]{:S(2)}) copy-start(s32[1,8]{1,0:T(1,128)} %top_hbm.1) | copy-start | bytes 100

commit v2 on v1

--- a/solution.py
+++ b/solution.py
@@ -106,17 +106,15 @@
 
     get_x.wait()
     get_basis.wait()
-    coefs = []
-    for l in range(LEAVES):
-        c = dot_nt(x_v[:, l * WIDTH : (l + 1) * WIDTH], basis_v[l]).astype(BF16)
-        coefs.append(c)
-        wide = c.astype(F32)
-        wide = jnp.concatenate([wide, wide], axis=1)
-        coef_send[0:NVEC, l, :] = wide
+    coefs = [
+        dot_nt(x_v[:, l * WIDTH : (l + 1) * WIDTH], basis_v[l]).astype(BF16) for l in range(LEAVES)
+    ]
+    for l in range(LEAVES):
+        wide = coefs[l].astype(F32)
+        coef_send[0:NVEC, l, :] = jnp.concatenate([wide, wide], axis=1)
     get_trans.wait()
-    partial = dot(coefs[0], trans_v[0])
-    for l in range(1, LEAVES):
-        partial = partial + dot(coefs[l], trans_v[l])
+    terms = [dot(coefs[l], trans_v[l]) for l in range(LEAVES)]
+    partial = functools.reduce(jnp.add, terms)
     coef_send[NVEC] = jnp.concatenate([partial, partial], axis=1)
 
     pl.semaphore_wait(barrier, TREES - 1 + SUBS - 1 + 2)
@@ -199,10 +197,11 @@
         [jnp.where(first == leaf_no, 1.0, 0.0), jnp.where(second == leaf_no, 1.0, 0.0)], axis=0
     ).astype(BF16)
     left = iota((64, 128), 1) < 64
+    boths = [
+        dot(onehot, coef_recv[:, v].reshape(SUBS * LEAVES, 128).astype(BF16)) for v in range(NVEC)
+    ]
     for v in range(NVEC):
-        source = coef_recv[:, v].reshape(SUBS * LEAVES, 128).astype(BF16)
-        both = dot(onehot, source)
-        picked_v[:, v, :] = jnp.where(left, both[0:64], both[64:128])
+        picked_v[:, v, :] = jnp.where(left, boths[v][0:64], boths[v][64:128])
     reply_send[...] = picked_v[...].astype(BF16)
     reply_recv[pl.ds(me, 1)] = reply_send[pl.ds(me, 1)]
 
@@ -236,24 +235,26 @@
     get_root.wait()
     get_top_s.wait()
     drain(node_recv.at[pl.ds(0, TREES - 1)], node_rsem)
-    root_local = None
+    terms = []
     for f in range(LINKS):
         n = node_recv[top_s[0, f]].astype(F32)
         n = jnp.concatenate([n[:, 0:64], n[:, 64:128]], axis=0).astype(BF16)
-        term = dot_nt(n, root_v[0, f])
-        root_local = term if root_local is None else root_local + term
+        terms.append(dot_nt(n, root_v[0, f]))
+    root_local = functools.reduce(jnp.add, terms)
     hi = root_local.astype(BF16)
     rest = root_local - hi.astype(F32)
     mid = rest.astype(BF16)
     lo = (rest - mid.astype(F32)).astype(BF16)
-    for l in range(LEAVES):
-        down_v[l] = (
-            dot_nt(hi, trans_v[l]) + dot_nt(mid, trans_v[l]) + dot_nt(lo, trans_v[l])
-        )
+    three = jnp.concatenate([hi, mid, lo], axis=0)
+    terms = [dot_nt(three, trans_v[l]) for l in range(LEAVES)]
+    for l in range(LEAVES):
+        t = terms[l]
+        down_v[l] = t[0:NVEC] + t[NVEC : 2 * NVEC] + t[2 * NVEC : 3 * NVEC]
 
     get_tree_s.wait()
     drain(reply_recv.at[pl.ds(0, TREES - 1)], reply_rsem)
     left = iota((NVEC, 128), 1) < 64
+    coefs = []
     for l in range(LEAVES):
         parts = []
         for f in range(0, LINKS, 2):
@@ -264,11 +265,13 @@
                 there = jnp.broadcast_to(rank_v[e : e + 1, :], (NVEC, 128)) == float(j)
                 halves.append(jnp.where(there, got, pltpu.roll(got, 64, 1)))
             parts.append(jnp.where(left, halves[0], halves[1]))
-        coef = jnp.concatenate(parts, axis=1).astype(BF16)
-        down = (dot_nt(coef, pairs_v[l]) + down_v[l]).astype(BF16)
-        out_ref[:, l * WIDTH : (l + 1) * WIDTH] = (
-            local_v[:, l * WIDTH : (l + 1) * WIDTH] + dot(down, basis_v[l])
-        ).astype(BF16)
+        coefs.append(jnp.concatenate(parts, axis=1).astype(BF16))
+    fars = [dot_nt(coefs[l], pairs_v[l]) for l in range(LEAVES)]
+    downs = [(fars[l] + down_v[l]).astype(BF16) for l in range(LEAVES)]
+    outs = [dot(downs[l], basis_v[l]) for l in range(LEAVES)]
+    for l in range(LEAVES):
+        here = slice(l * WIDTH, (l + 1) * WIDTH)
+        out_ref[:, here] = (local_v[:, here] + outs[l]).astype(BF16)
 
     to_after.wait_send()
     to_before.wait_send()
@@ -332,7 +335,7 @@
         out_specs=pl.BlockSpec(memory_space=pltpu.VMEM),
         scratch_shapes=scratch,
         compiler_params=pltpu.CompilerParams(
-            collective_id=0, has_side_effects=True, vmem_limit_bytes=32 * 2**20
+            collective_id=0, has_side_effects=True, vmem_limit_bytes=60 * 2**20
         ),
         name="product",
     )(vectors, basis, near, transfer, tree, offset, far, top, root)

time: 35.7 us -> 27.3 us (0.76)
  local copies, waits for them, and re-layouts: 9.27 us -> 1.38 us
    unnamed x19 -> x1, local copies, waits for them, and re-layouts: 9.27 us -> 1.38 us
where the time goes in v2:
time: 27.3 us; the launch traced here: 27.2 us
  Pallas kernels  25.8 us (95%)
  local copies, waits for them, and re-layouts  1.38 us (5%)
    pallas_call x1, Pallas kernels, shards(): pl.pallas_call(kernel, out_shape=jax.ShapeDtypeStruct(vectors.shape, BF16...  25.8 us
    unnamed x1, local copies, waits for them, and re-layouts  1.38 us

profile of v2, /device:TPU:1, one launch (start us, length us, event | category | flops | bytes accessed | tf_op | source)
XLA Modules:
  0.0 27.2 jit_solution(6298721979057148169)
XLA Ops:
  0.0 25.8 %product.1 = bf16[8,2048]{1,0:T(8,128)(2,1)} custom-call(bf16[8,2048]{1,0:T(8,128)(2,1)} %vec_hbm.1, bf16[8,64,256]{2,1,0:T(8,128)(2,1)} %basis_hbm.1, bf16[8,256,768]{2,1,0:T(8,128)(2,1)} %near_hbm.1, bf16[8,64,64]{2,1,0:T(8,128)(2,1)} %trans_hbm.1, s32[8,8]{1,0:T(8,128)} %tree_hbm.1, s32[8,8]{1,0:T(8,128)} %offset_hbm.1, bf16[8,8,64,64]{3,2,1,0:T(8,128)(2,1)} %far_hbm.1, ...), custom_call_target="tpu_custom_call" | custom-call | tf_op jit(solution)/shard_map/product/pallas_call | solution.py:331
  25.8 1.4 %copy.11 = bf16[8,2048]{1,0:T(8,128)(2,1)} copy(bf16[8,2048]{1,0:T(8,128)(2,1)} %product.1) | data formatting | bytes 65536

commit v3 on v2

v3 whole, which is shorter than its diff:
```python
import functools

import jax
import jax.numpy as jnp
from jax import lax
from jax.experimental import pallas as pl
from jax.experimental.pallas import tpu as pltpu
from jax.sharding import PartitionSpec as P

MESH = pl.DeviceIdType.MESH
F32 = jnp.float32
BF16 = jnp.bfloat16
NT = (((1,), (1,)), ((), ()))
TREES = 64
SUBS = 4
LEAVES = 8
LINKS = 8
NVEC = 8
RANK = 64
WIDTH = 256
HOMES = 32


def dot(a, b):
    return jnp.dot(a, b, preferred_element_type=F32)


def dot_nt(a, b):
    return lax.dot_general(a, b, NT, preferred_element_type=F32)


def iota(shape, dim):
    return lax.broadcasted_iota(jnp.int32, shape, dim)


def drain(ref, sem):
    pltpu.make_async_copy(ref, ref, sem).wait()


def mirror(leaf):
    return leaf + 14 - 4 * lax.rem(leaf // 2, 8)


def home_leaf(j):
    return (j // 8) * 16 + lax.rem(j, 8)


def slot_of(tree):
    m = tree & 15
    late = m >> 3
    return (late * HOMES + ((tree >> 4) << 3) + ((m ^ (late * 14)) & 7)) & (2 * HOMES - 1)


def kernel(
    vec_hbm, basis_hbm, near_hbm, trans_hbm, tree_hbm, offset_hbm, far_hbm, top_hbm, root_hbm,
    out_ref,
    x_v, basis_v, near_v, trans_v, tree_v, offset_v, far_v, root_v, top_v, slot_v, top_slot_v, client_v,
    slot_s, top_slot_s, client_s,
    table_send, table_recv, coef_send, coef_recv, part_send, part_recv, wide_v, both_v, plan_v,
    node_send, node_recv, node_mine, node_theirs, halo_v,
    reply_send, reply_recv, picked_v, rank_v, pairs_v, down_v, local_v,
    sem_x, sem_basis, sem_near, sem_trans, sem_table, sem_far, sem_root, sem_smem,
    halo_ssem, halo_rsem, table_ssem, table_rsem, coef_ssem, coef_rsem, part_ssem, part_rsem,
    node_ssem, node_rsem, reply_ssem, reply_rsem, fwd_sem, pick_sem, client_sem,
):
    me = lax.axis_index("leaf")
    sub = lax.axis_index("sub")
    late = lax.rem(me, 16) // 8
    other = mirror(me)
    home = me + late * (other - me)
    j = (home // 16) * 8 + lax.rem(home, 16)

    def step(leaf, s, by):
        flat = lax.rem(leaf * SUBS + s + by + TREES * SUBS, TREES * SUBS)
        return flat // SUBS, lax.rem(flat, SUBS)

    def home_of(leaf):
        late = lax.rem(leaf, 16) // 8
        return leaf + late * (mirror(leaf) - leaf), late

    barrier = pltpu.get_barrier_semaphore()

    def announce(leaf, s):
        pl.semaphore_signal(
            barrier, inc=1, device_id={"leaf": leaf, "sub": s}, device_id_type=MESH
        )

    def send(src, dst, ssem, rsem, leaf, s):
        pltpu.make_async_remote_copy(
            src_ref=src, dst_ref=dst, send_sem=ssem, recv_sem=rsem,
            device_id={"leaf": leaf, "sub": s}, device_id_type=MESH,
        ).start()

    for i in range(1, SUBS):
        announce(me, lax.rem(sub + i, SUBS))

    @pl.when(late == 0)
    def _():
        def greet(i, carry):
            announce(lax.rem(me + i, TREES), sub)
            return carry

        for leaf in (me, other):
            for by in (-1, 1):
                announce(*step(leaf, sub, by))
        lax.fori_loop(1, TREES, greet, 0)
        for i in range(1, SUBS):
            announce(other, lax.rem(sub + i, SUBS))

    @pl.when(late == 1)
    def _():
        def greet(i, carry):
            announce(mirror(home_leaf(lax.rem(j + i, HOMES))), sub)
            return carry

        lax.fori_loop(1, HOMES, greet, 0)

    get_tree = pltpu.make_async_copy(tree_hbm, tree_v, sem_table.at[0])
    get_offset = pltpu.make_async_copy(offset_hbm, offset_v, sem_table.at[1])
    get_top = pltpu.make_async_copy(top_hbm, top_v, sem_table.at[2])
    get_x = pltpu.make_async_copy(vec_hbm, x_v, sem_x)
    get_basis = pltpu.make_async_copy(basis_hbm, basis_v, sem_basis)
    get_trans = pltpu.make_async_copy(trans_hbm, trans_v, sem_trans)
    get_far = pltpu.make_async_copy(far_hbm, far_v, sem_far)
    get_root = pltpu.make_async_copy(root_hbm, root_v, sem_root)
    get_near = [
        pltpu.make_async_copy(near_hbm.at[l], near_v.at[l], sem_near.at[l]) for l in range(LEAVES)
    ]
    for copy in (get_tree, get_offset, get_top, get_x, get_basis, get_trans):
        copy.start()
    get_far.start()
    get_root.start()
    for copy in get_near:
        copy.start()

    get_tree.wait()
    get_offset.wait()
    get_top.wait()
    slot_v[...] = slot_of(tree_v[...])
    top_slot_v[...] = slot_of(top_v[...])
    get_slot = pltpu.make_async_copy(slot_v, slot_s, sem_smem.at[0])
    get_top_slot = pltpu.make_async_copy(top_slot_v, top_slot_s, sem_smem.at[1])
    get_slot.start()
    get_top_slot.start()
    tree = tree_v[...].astype(F32).astype(BF16)
    offset = offset_v[...].astype(F32).astype(BF16)
    lane = iota((LINKS, 128), 1)
    column = iota((LINKS, 128), 0)
    low = jnp.where((lax.rem(lane, LINKS) == column) & (lane < 64), 1.0, 0.0).astype(BF16)
    rows = dot(tree, low) * 32.0 + dot(offset, low)
    own_row = lane // LINKS == column
    table_row = jnp.sum(jnp.where(own_row, rows, 0.0), axis=0, keepdims=True)
    table_row = table_row.astype(jnp.int32)
    table_send[...] = table_row

    get_x.wait()
    get_basis.wait()
    coefs = [
        dot_nt(x_v[:, l * WIDTH : (l + 1) * WIDTH], basis_v[l]).astype(BF16) for l in range(LEAVES)
    ]
    for l in range(0, LEAVES, 2):
        coef_send[l // 2] = jnp.concatenate(
            [coefs[l].astype(F32), coefs[l + 1].astype(F32)], axis=1
        ).astype(BF16)
    get_trans.wait()
    terms = [dot(coefs[l], trans_v[l]) for l in range(LEAVES)]
    partial = functools.reduce(jnp.add, terms)
    part_send[...] = jnp.concatenate([partial[0 : NVEC // 2], partial[NVEC // 2 :]], axis=1)

    def send_coefs(leaf, s):
        send(coef_send, coef_recv.at[late * SUBS + sub], coef_ssem, coef_rsem.at[late], leaf, s)
        send(part_send, part_recv.at[late, sub], part_ssem, part_rsem.at[late], leaf, s)

    @pl.when(late == 0)
    def _():
        pl.semaphore_wait(barrier, HOMES - 1 + SUBS - 1 + 2)
        for i in range(1, SUBS):
            send_coefs(me, lax.rem(sub + i, SUBS))
        coef_recv[pl.ds(sub, 1)] = coef_send[...][None]
        part_recv[0, pl.ds(sub, 1)] = part_send[...][None]

    @pl.when(late == 1)
    def _():
        pl.semaphore_wait(barrier, 2 * HOMES - 1 + 2 * (SUBS - 1) + 2)
        for i in range(SUBS):
            send_coefs(other, lax.rem(sub + i, SUBS))
        for i in range(1, SUBS):
            send(
                coef_send, coef_recv.at[SUBS + sub], coef_ssem, coef_rsem.at[1],
                me, lax.rem(sub + i, SUBS),
            )
        coef_recv[pl.ds(SUBS + sub, 1)] = coef_send[...][None]

    @pl.when(late == 0)
    def _():
        table_recv[pl.ds(j, 1)] = table_send[...][None]

        def ask(i, carry):
            leaf = home_leaf(lax.rem(j + i, HOMES))
            send(table_send, table_recv.at[j], table_ssem, table_rsem.at[0], leaf, sub)
            return carry

        lax.fori_loop(1, HOMES, ask, 0)

    @pl.when(late == 1)
    def _():
        def ask(i, carry):
            leaf = home_leaf(lax.rem(j + i, HOMES))
            send(table_send, table_recv.at[HOMES + j], table_ssem, table_rsem.at[1], leaf, sub)
            return carry

        def ask_late(i, carry):
            leaf = mirror(home_leaf(lax.rem(j + i, HOMES)))
            send(table_send, table_recv.at[HOMES + j], table_ssem, table_rsem.at[1], leaf, sub)
            return carry

        send(top_slot_v, client_v, client_sem.at[0], client_sem.at[1], other, sub)
        lax.fori_loop(0, HOMES, ask, 0)
        lax.fori_loop(1, HOMES, ask_late, 0)
        table_recv[pl.ds(HOMES + j, 1)] = table_send[...][None]

    for side, by, start in ((0, 1, (LEAVES - 1) * WIDTH), (1, -1, 0)):
        leaf, s = step(me, sub, by)
        leaf, kind = home_of(leaf)
        send(
            vec_hbm.at[:, pl.ds(start, WIDTH)], halo_v.at[kind, side],
            halo_ssem, halo_rsem.at[kind, side], leaf, s,
        )

    entry = iota((64, LINKS), 0)
    link = iota((64, LINKS), 1)
    pick_row = jnp.where(entry // LINKS == link, 1.0, 0.0).astype(BF16)
    by_entry = dot(pick_row, tree)
    tree_col = jnp.sum(
        jnp.where(lax.rem(entry, LINKS) == link, by_entry, 0.0), axis=1, keepdims=True
    )
    tree_row = (table_row[:, 0:64] >> 5).astype(F32)
    same = (tree_col == tree_row) & (iota((64, 64), 1) < iota((64, 64), 0))
    rank_col = jnp.sum(jnp.where(same, 1.0, 0.0), axis=1, keepdims=True)
    rank_v[...] = jnp.broadcast_to(rank_col, (64, 128))

    get_far.wait()
    for l in range(LEAVES):
        for f in range(0, LINKS, 2):
            pairs_v[l, :, f * RANK : (f + 2) * RANK] = jnp.concatenate(
                [far_v[l, f], far_v[l, f + 1]], axis=1
            )

    def near(l, before, after):
        middle = x_v[:, l * WIDTH : (l + 1) * WIDTH]
        span = jnp.concatenate([before, middle, after], axis=1)
        local_v[:, l * WIDTH : (l + 1) * WIDTH] = dot_nt(span, near_v[l])

    for l in range(1, LEAVES - 1):
        get_near[l].wait()
        near(l, x_v[:, (l - 1) * WIDTH : l * WIDTH], x_v[:, (l + 1) * WIDTH : (l + 2) * WIDTH])
    get_near[0].wait()
    get_near[LEAVES - 1].wait()
    get_root.wait()
    get_slot.wait()
    get_top_slot.wait()

    earlier = jnp.where(iota((64, 64), 0) < iota((64, 64), 1), 1.0, 0.0).astype(BF16)
    row_no = iota((HOMES, SUBS * LEAVES), 1) + 1

    def plan(kind, asker, tree_id):
        table = table_recv[asker * HOMES : (asker + 1) * HOMES, 0, :][:, 0:64]
        asked = (table >> 5) == tree_id
        pair = (table & 31) >> 1
        odd = table & 1
        order = dot(jnp.where(asked, 1.0, 0.0).astype(BF16), earlier)
        rows = (
            jnp.where(asked & (order == 0.0), (pair + 16 * odd + 1).astype(F32), 0.0),
            jnp.where(asked & (order == 1.0), (pair + 16 - 16 * odd + 1).astype(F32), 0.0),
        )
        plan_v[2 * asker + kind] = jnp.concatenate(
            [
                jnp.where(
                    jnp.sum(r, axis=1, keepdims=True).astype(jnp.int32) == row_no, 1.0, 0.0
                )
                for r in rows
            ],
            axis=0,
        ).astype(BF16)

    def fill(kind, asker):
        at = 2 * asker + kind
        left = iota((HOMES, 128), 1) < 64
        onehot = plan_v[at]
        boths = [dot(onehot, both_v[kind, v]) for v in range(NVEC)]
        for v in range(NVEC):
            picked_v[at, :, v, :] = jnp.where(left, boths[v][0:HOMES], boths[v][HOMES:])
        reply_send[at * HOMES : (at + 1) * HOMES] = picked_v[at].astype(BF16)

    def sums(kind):
        node = functools.reduce(jnp.add, [part_recv[kind, i] for i in range(SUBS)]).astype(BF16)
        node_send[kind] = node
        node_recv[pl.ds(kind * HOMES + j, 1)] = node[None]

    def unpack(kind):
        pairs = coef_recv[kind * SUBS : (kind + 1) * SUBS]
        wide_v[kind] = pairs.reshape(SUBS * LEAVES // 2, NVEC, 128).astype(F32)
        for v in range(NVEC):
            straight = wide_v[kind, :, v, :]
            turned = pltpu.roll(straight, 64, 1)
            both_v[kind, v] = jnp.concatenate([straight, turned], axis=0).astype(BF16)

    def spread_nodes(kind):
        def one(i, carry):
            leaf = home_leaf(lax.rem(j + i, HOMES))
            send(node_send.at[kind], node_recv.at[kind * HOMES + j], node_ssem, node_rsem, leaf, sub)
            return carry

        lax.fori_loop(1, HOMES, one, 0)

    def reply(kind, asker):
        def one(i, carry):
            to = lax.rem(j + i, HOMES)
            leaf = home_leaf(to)
            if asker:
                leaf = mirror(leaf)
            send(
                reply_send.at[(2 * asker + kind) * HOMES + to], reply_recv.at[kind * HOMES + j],
                reply_ssem, reply_rsem, leaf, sub,
            )
            return carry

        lax.fori_loop(0 if kind < asker else 1, HOMES, one, 0)
        if kind >= asker:
            reply_recv[pl.ds(kind * HOMES + j, 1)] = reply_send[
                pl.ds((2 * asker + kind) * HOMES + j, 1)
            ]

    def near_ends():
        zero = jnp.zeros((NVEC, WIDTH), BF16)
        first = (me == 0) & (sub == 0)
        last = (me == TREES - 1) & (sub == SUBS - 1)
        near(0, jnp.where(first, zero, halo_v[0, 0]), x_v[:, WIDTH : 2 * WIDTH])
        near(
            LEAVES - 1,
            x_v[:, (LEAVES - 2) * WIDTH : (LEAVES - 1) * WIDTH],
            jnp.where(last, zero, halo_v[0, 1]),
        )

    @pl.when(late == 0)
    def _():
        drain(part_recv.at[0, pl.ds(0, SUBS - 1)], part_rsem.at[0])
        sums(0)
        spread_nodes(0)
        drain(coef_recv.at[pl.ds(0, SUBS - 1)], coef_rsem.at[0])
        unpack(0)
        drain(table_recv.at[pl.ds(0, HOMES - 1)], table_rsem.at[0])
        plan(0, 0, me)
        fill(0, 0)
        reply(0, 0)
        plan(1, 0, other)
        drain(part_recv.at[1], part_rsem.at[1])
        sums(1)
        spread_nodes(1)
        drain(coef_recv.at[pl.ds(SUBS, SUBS)], coef_rsem.at[1])
        unpack(1)
        fill(1, 0)
        reply(1, 0)
        drain(table_recv.at[pl.ds(0, HOMES)], table_rsem.at[1])
        drain(client_v, client_sem.at[1])
        get_client = pltpu.make_async_copy(client_v, client_s, sem_smem.at[0])
        get_client.start()
        plan(0, 1, me)
        fill(0, 1)
        reply(0, 1)
        for kind in range(2):
            for side in range(2):
                drain(halo_v.at[kind, side], halo_rsem.at[kind, side])
        send(halo_v.at[1], halo_v.at[0], fwd_sem.at[0], fwd_sem.at[1], other, sub)
        near_ends()
        get_client.wait()
        drain(node_recv.at[pl.ds(0, 2 * HOMES - 2)], node_rsem)
        for f in range(LINKS):
            node_theirs[f] = node_recv[client_s[0, f]]
        send(node_theirs, node_mine, pick_sem.at[0], pick_sem.at[1], other, sub)
        for f in range(LINKS):
            node_mine[f] = node_recv[top_slot_s[0, f]]

    @pl.when(late == 1)
    def _():
        drain(coef_recv.at[pl.ds(0, SUBS - 1)], coef_rsem.at[1])
        unpack(1)
        drain(table_recv.at[pl.ds(0, HOMES - 1)], table_rsem.at[1])
        plan(1, 1, me)
        fill(1, 1)
        reply(1, 1)
        drain(halo_v.at[0], fwd_sem.at[1])
        near_ends()
        drain(node_mine, pick_sem.at[1])

    terms = []
    for f in range(LINKS):
        n = node_mine[f].astype(F32)
        n = jnp.concatenate([n[:, 0:64], n[:, 64:128]], axis=0).astype(BF16)
        terms.append(dot_nt(n, root_v[0, f]))
    root_local = functools.reduce(jnp.add, terms)
    hi = root_local.astype(BF16)
    rest = root_local - hi.astype(F32)
    mid = rest.astype(BF16)
    lo = (rest - mid.astype(F32)).astype(BF16)
    three = jnp.concatenate([hi, mid, lo], axis=0)
    terms = [dot_nt(three, trans_v[l]) for l in range(LEAVES)]
    for l in range(LEAVES):
        t = terms[l]
        down_v[l] = t[0:NVEC] + t[NVEC : 2 * NVEC] + t[2 * NVEC : 3 * NVEC]

    @pl.when(late == 0)
    def _():
        drain(reply_recv.at[pl.ds(0, 2 * HOMES - 2)], reply_rsem)

    @pl.when(late == 1)
    def _():
        drain(reply_recv.at[pl.ds(0, 2 * HOMES - 1)], reply_rsem)

    left = iota((NVEC, 128), 1) < 64
    coefs = []
    for l in range(LEAVES):
        parts = []
        for f in range(0, LINKS, 2):
            halves = []
            for k in range(2):
                e = l * LINKS + f + k
                got = reply_recv[slot_s[l, f + k]].astype(F32)
                there = jnp.broadcast_to(rank_v[e : e + 1, :], (NVEC, 128)) == float(k)
                halves.append(jnp.where(there, got, pltpu.roll(got, 64, 1)))
            parts.append(jnp.where(left, halves[0], halves[1]))
        coefs.append(jnp.concatenate(parts, axis=1).astype(BF16))
    fars = [dot_nt(coefs[l], pairs_v[l]) for l in range(LEAVES)]
    downs = [(fars[l] + down_v[l]).astype(BF16) for l in range(LEAVES)]
    outs = [dot(downs[l], basis_v[l]) for l in range(LEAVES)]
    for l in range(LEAVES):
        here = slice(l * WIDTH, (l + 1) * WIDTH)
        out_ref[:, here] = (local_v[:, here] + outs[l]).astype(BF16)

    drain(halo_v.at[0], halo_ssem)

    @pl.when(late == 0)
    def _():
        drain(coef_recv.at[pl.ds(0, SUBS - 1)], coef_ssem)
        drain(part_recv.at[0, pl.ds(0, SUBS - 1)], part_ssem)
        drain(table_recv.at[pl.ds(0, HOMES - 1)], table_ssem)
        drain(node_recv.at[pl.ds(0, 2 * HOMES - 2)], node_ssem)
        drain(reply_send.at[pl.ds(0, 3 * HOMES - 2)], reply_ssem)
        drain(halo_v.at[1], fwd_sem.at[0])
        drain(node_theirs, pick_sem.at[0])

    @pl.when(late == 1)
    def _():
        drain(coef_recv.at[pl.ds(0, 2 * SUBS - 1)], coef_ssem)
        drain(part_recv.at[0], part_ssem)
        drain(table_recv.at[pl.ds(0, 2 * HOMES - 1)], table_ssem)
        drain(client_v, client_sem.at[0])
        drain(reply_send.at[pl.ds(0, HOMES - 1)], reply_ssem)


def shards(vectors, basis, near, transfer, tree, offset, far, top, root):
    dma = pltpu.SemaphoreType.DMA
    i32 = jnp.int32
    scratch = [
        pltpu.VMEM((NVEC, LEAVES * WIDTH), BF16),
        pltpu.VMEM((LEAVES, RANK, WIDTH), BF16),
        pltpu.VMEM((LEAVES, WIDTH, 3 * WIDTH), BF16),
        pltpu.VMEM((LEAVES, RANK, RANK), BF16),
        pltpu.VMEM((LEAVES, LINKS), i32),
        pltpu.VMEM((LEAVES, LINKS), i32),
        pltpu.VMEM((LEAVES, LINKS, RANK, RANK), BF16),
        pltpu.VMEM((1, LINKS, RANK, RANK), BF16),
        pltpu.VMEM((1, LINKS), i32),
        pltpu.VMEM((LEAVES, LINKS), i32),
        pltpu.VMEM((1, LINKS), i32),
        pltpu.VMEM((1, LINKS), i32),
        pltpu.SMEM((LEAVES, LINKS), i32),
        pltpu.SMEM((1, LINKS), i32),
        pltpu.SMEM((1, LINKS), i32),
        pltpu.VMEM((1, 128), i32),
        pltpu.VMEM((2 * HOMES, 1, 128), i32),
        pltpu.VMEM((LEAVES // 2, NVEC, 128), BF16),
        pltpu.VMEM((2 * SUBS, LEAVES // 2, NVEC, 128), BF16),
        pltpu.VMEM((NVEC // 2, 128), F32),
        pltpu.VMEM((2, SUBS, NVEC // 2, 128), F32),
        pltpu.VMEM((2, SUBS * LEAVES // 2, NVEC, 128), F32),
        pltpu.VMEM((2, NVEC, SUBS * LEAVES, 128), BF16),
        pltpu.VMEM((4, 2 * HOMES, SUBS * LEAVES), BF16),
        pltpu.VMEM((2, NVEC // 2, 128), BF16),
        pltpu.VMEM((2 * HOMES, NVEC // 2, 128), BF16),
        pltpu.VMEM((LINKS, NVEC // 2, 128), BF16),
        pltpu.VMEM((LINKS, NVEC // 2, 128), BF16),
        pltpu.VMEM((2, 2, NVEC, WIDTH), BF16),
        pltpu.VMEM((4 * HOMES, NVEC, 128), BF16),
        pltpu.VMEM((2 * HOMES, NVEC, 128), BF16),
        pltpu.VMEM((4, HOMES, NVEC, 128), F32),
        pltpu.VMEM((64, 128), F32),
        pltpu.VMEM((LEAVES, RANK, LINKS * RANK), BF16),
        pltpu.VMEM((LEAVES, NVEC, RANK), F32),
        pltpu.VMEM((NVEC, LEAVES * WIDTH), F32),
        dma,
        dma,
        dma((LEAVES,)),
        dma,
        dma((3,)),
        dma,
        dma,
        dma((2,)),
        dma,
        dma((2, 2)),
        dma,
        dma((2,)),
        dma,
        dma((2,)),
        dma,
        dma((2,)),
        dma,
        dma,
        dma,
        dma,
        dma((2,)),
        dma((2,)),
        dma((2,)),
    ]
    return pl.pallas_call(
        kernel,
        out_shape=jax.ShapeDtypeStruct(vectors.shape, BF16),
        in_specs=[pl.BlockSpec(memory_space=pl.ANY)] * 9,
        out_specs=pl.BlockSpec(memory_space=pltpu.VMEM),
        scratch_shapes=scratch,
        compiler_params=pltpu.CompilerParams(
            collective_id=0, has_side_effects=True, vmem_limit_bytes=40 * 2**20
        ),
        name="product",
    )(*[
        pltpu.with_memory_space_constraint(a, pltpu.HBM)
        for a in (vectors, basis, near, transfer, tree, offset, far, top, root)
    ])


def solution(mesh):
    placed = (
        P(None, ("leaf", "sub")),
        P(("leaf", "sub"), None, None),
        P(("leaf", "sub"), None, None),
        P(("leaf", "sub"), None, None),
        P(("leaf", "sub"), None),
        P(("leaf", "sub"), None),
        P(("leaf", "sub"), None, None, None),
        P("leaf", None),
        P("leaf", None, None, None),
    )
    return jax.shard_map(
        shards, mesh=mesh, in_specs=placed, out_specs=P(None, ("leaf", "sub")), check_vma=False
    )
```

time: 27.3 us -> 24.5 us (0.90)
  Pallas kernels: 25.8 us -> 23.8 us
  local copies, waits for them, and re-layouts: 1.38 us -> 0.62 us
    pallas_call x1, Pallas kernels: 25.8 us -> 23.8 us  [shards(): pl.pallas_call(kernel, out_shape=jax.ShapeDtypeStruct(vectors.shape, BF16...]
    unnamed x1, local copies, waits for them, and re-layouts: 1.38 us -> 0.62 us
where the time goes in v3:
time: 24.5 us; the launch traced here: 24.4 us
  Pallas kernels  23.8 us (97%)
  local copies, waits for them, and re-layouts  0.62 us (3%)
    pallas_call x1, Pallas kernels, shards(): pl.pallas_call(kernel, out_shape=jax.ShapeDtypeStruct(vectors.shape, BF16...  23.8 us
    unnamed x1, local copies, waits for them, and re-layouts  0.62 us

profile of v3, /device:TPU:1, one launch (start us, length us, event | category | flops | bytes accessed | tf_op | source)
XLA Modules:
  0.0 24.4 jit_solution(3469701127514285732)
XLA Ops:
  0.0 23.8 %product.1 = bf16[8,2048]{1,0:T(8,128)(2,1)S(1)} custom-call(bf16[8,2048]{1,0:T(8,128)(2,1)} %vec_hbm.1, bf16[8,64,256]{2,1,0:T(8,128)(2,1)} %basis_hbm.1, bf16[8,256,768]{2,1,0:T(8,128)(2,1)} %near_hbm.1, bf16[8,64,64]{2,1,0:T(8,128)(2,1)} %trans_hbm.1, s32[8,8]{1,0:T(8,128)} %tree_hbm.1, s32[8,8]{1,0:T(8,128)} %offset_hbm.1, ...), custom_call_target="tpu_custom_call" | custom-call | tf_op jit(solution)/shard_map/product/pallas_call | solution.py:525
  23.8 0.6 %copy.11 = bf16[8,2048]{1,0:T(8,128)(2,1)} copy(bf16[8,2048]{1,0:T(8,128)(2,1)S(1)} %product.1) | data formatting | bytes 65536

commit v4 on v3

--- a/solution.py
+++ b/solution.py
@@ -42,13 +42,15 @@
 
 
 def home_leaf(j):
-    return (j // 8) * 16 + lax.rem(j, 8)
+    return (lax.rem(j, 8) // 2) * 16 + (j // 8) * 2 + lax.rem(j, 2)
 
 
 def slot_of(tree):
     m = tree & 15
     late = m >> 3
-    return (late * HOMES + ((tree >> 4) << 3) + ((m ^ (late * 14)) & 7)) & (2 * HOMES - 1)
+    m = (m ^ (late * 14)) & 7
+    j = ((m >> 1) << 3) + ((tree >> 4) << 1) + (m & 1)
+    return (late * HOMES + j) & (2 * HOMES - 1)
 
 
 def kernel(
@@ -61,14 +63,15 @@
     reply_send, reply_recv, picked_v, rank_v, pairs_v, down_v, local_v,
     sem_x, sem_basis, sem_near, sem_trans, sem_table, sem_far, sem_root, sem_smem,
     halo_ssem, halo_rsem, table_ssem, table_rsem, coef_ssem, coef_rsem, part_ssem, part_rsem,
-    node_ssem, node_rsem, reply_ssem, reply_rsem, fwd_sem, pick_sem, client_sem,
+    node_ssem, node_rsem, reply_ssem, reply_rsem, fwd_sem, pick_sem, client_sem, pass_sem,
 ):
     me = lax.axis_index("leaf")
     sub = lax.axis_index("sub")
     late = lax.rem(me, 16) // 8
     other = mirror(me)
     home = me + late * (other - me)
-    j = (home // 16) * 8 + lax.rem(home, 16)
+    j = (lax.rem(home, 16) // 2) * 8 + (home // 16) * 2 + lax.rem(home, 2)
+    row = j - lax.rem(j, 8)
 
     def step(leaf, s, by):
         flat = lax.rem(leaf * SUBS + s + by + TREES * SUBS, TREES * SUBS)
@@ -91,29 +94,34 @@
             device_id={"leaf": leaf, "sub": s}, device_id_type=MESH,
         ).start()
 
-    for i in range(1, SUBS):
-        announce(me, lax.rem(sub + i, SUBS))
-
     @pl.when(late == 0)
     def _():
+        def greet_late(i, carry):
+            y, c = lax.rem(i, 8) // 2, lax.rem(i, 2)
+            announce(lax.rem(me // 16 + y, 4) * 16 + (7 - i // 8) * 2 + c, sub)
+            return carry
+
         def greet(i, carry):
-            announce(lax.rem(me + i, TREES), sub)
+            announce(home_leaf(lax.rem(j + i, HOMES)), sub)
             return carry
 
+        for i in range(1, SUBS):
+            announce(other, lax.rem(sub + i, SUBS))
         for leaf in (me, other):
             for by in (-1, 1):
                 announce(*step(leaf, sub, by))
-        lax.fori_loop(1, TREES, greet, 0)
-        for i in range(1, SUBS):
-            announce(other, lax.rem(sub + i, SUBS))
-
-    @pl.when(late == 1)
-    def _():
-        def greet(i, carry):
-            announce(mirror(home_leaf(lax.rem(j + i, HOMES))), sub)
-            return carry
-
-        lax.fori_loop(1, HOMES, greet, 0)
+        lax.fori_loop(0, HOMES, greet_late, 0, unroll=True)
+        lax.fori_loop(1, HOMES, greet, 0, unroll=True)
+
+    @pl.when(late == 1)
+    def _():
+        for i in range(1, 4):
+            announce(mirror(home_leaf(lax.rem(j + 8 * i, HOMES))), sub)
+        for i in range(1, 8):
+            announce(mirror(home_leaf(row + lax.rem(j + i, 8))), sub)
+
+    for i in range(1, SUBS):
+        announce(me, lax.rem(sub + i, SUBS))
 
     get_tree = pltpu.make_async_copy(tree_hbm, tree_v, sem_table.at[0])
     get_offset = pltpu.make_async_copy(offset_hbm, offset_v, sem_table.at[1])
@@ -167,13 +175,17 @@
     partial = functools.reduce(jnp.add, terms)
     part_send[...] = jnp.concatenate([partial[0 : NVEC // 2], partial[NVEC // 2 :]], axis=1)
 
+    def send_part(leaf, s):
+        send(part_send, part_recv.at[late, sub], part_ssem, part_rsem.at[late], leaf, s)
+
     def send_coefs(leaf, s):
         send(coef_send, coef_recv.at[late * SUBS + sub], coef_ssem, coef_rsem.at[late], leaf, s)
-        send(part_send, part_recv.at[late, sub], part_ssem, part_rsem.at[late], leaf, s)
 
     @pl.when(late == 0)
     def _():
         pl.semaphore_wait(barrier, HOMES - 1 + SUBS - 1 + 2)
+        for i in range(1, SUBS):
+            send_part(me, lax.rem(sub + i, SUBS))
         for i in range(1, SUBS):
             send_coefs(me, lax.rem(sub + i, SUBS))
         coef_recv[pl.ds(sub, 1)] = coef_send[...][None]
@@ -181,7 +193,9 @@
 
     @pl.when(late == 1)
     def _():
-        pl.semaphore_wait(barrier, 2 * HOMES - 1 + 2 * (SUBS - 1) + 2)
+        pl.semaphore_wait(barrier, HOMES + 7 + 3 + 2 * (SUBS - 1) + 2)
+        for i in range(SUBS):
+            send_part(other, lax.rem(sub + i, SUBS))
         for i in range(SUBS):
             send_coefs(other, lax.rem(sub + i, SUBS))
         for i in range(1, SUBS):
@@ -200,7 +214,7 @@
             send(table_send, table_recv.at[j], table_ssem, table_rsem.at[0], leaf, sub)
             return carry
 
-        lax.fori_loop(1, HOMES, ask, 0)
+        lax.fori_loop(1, HOMES, ask, 0, unroll=True)
 
     @pl.when(late == 1)
     def _():
@@ -209,14 +223,11 @@
             send(table_send, table_recv.at[HOMES + j], table_ssem, table_rsem.at[1], leaf, sub)
             return carry
 
-        def ask_late(i, carry):
-            leaf = mirror(home_leaf(lax.rem(j + i, HOMES)))
+        send(top_slot_v, client_v, client_sem.at[0], client_sem.at[1], other, sub)
+        for i in range(1, 8):
+            leaf = mirror(home_leaf(row + lax.rem(j + i, 8)))
             send(table_send, table_recv.at[HOMES + j], table_ssem, table_rsem.at[1], leaf, sub)
-            return carry
-
-        send(top_slot_v, client_v, client_sem.at[0], client_sem.at[1], other, sub)
         lax.fori_loop(0, HOMES, ask, 0)
-        lax.fori_loop(1, HOMES, ask_late, 0)
         table_recv[pl.ds(HOMES + j, 1)] = table_send[...][None]
 
     for side, by, start in ((0, 1, (LEAVES - 1) * WIDTH), (1, -1, 0)):
@@ -259,6 +270,14 @@
     get_root.wait()
     get_slot.wait()
     get_top_slot.wait()
+
+    @pl.when(late == 1)
+    def _():
+        drain(table_recv.at[pl.ds(0, 7)], table_rsem.at[1])
+        rows = table_recv.at[pl.ds(HOMES + row, 8)]
+        for i in range(1, 4):
+            leaf = mirror(home_leaf(lax.rem(j + 8 * i, HOMES)))
+            send(rows, rows, pass_sem.at[0], pass_sem.at[1], leaf, sub)
 
     earlier = jnp.where(iota((64, 64), 0) < iota((64, 64), 1), 1.0, 0.0).astype(BF16)
     row_no = iota((HOMES, SUBS * LEAVES), 1) + 1
@@ -311,7 +330,7 @@
             send(node_send.at[kind], node_recv.at[kind * HOMES + j], node_ssem, node_rsem, leaf, sub)
             return carry
 
-        lax.fori_loop(1, HOMES, one, 0)
+        lax.fori_loop(1, HOMES, one, 0, unroll=True)
 
     def reply(kind, asker):
         def one(i, carry):
@@ -325,7 +344,7 @@
             )
             return carry
 
-        lax.fori_loop(0 if kind < asker else 1, HOMES, one, 0)
+        lax.fori_loop(0 if kind < asker else 1, HOMES, one, 0, unroll=True)
         if kind >= asker:
             reply_recv[pl.ds(kind * HOMES + j, 1)] = reply_send[
                 pl.ds((2 * asker + kind) * HOMES + j, 1)
@@ -351,9 +370,9 @@
         unpack(0)
         drain(table_recv.at[pl.ds(0, HOMES - 1)], table_rsem.at[0])
         plan(0, 0, me)
+        plan(1, 0, other)
         fill(0, 0)
         reply(0, 0)
-        plan(1, 0, other)
         drain(part_recv.at[1], part_rsem.at[1])
         sums(1)
         spread_nodes(1)
@@ -385,7 +404,7 @@
     def _():
         drain(coef_recv.at[pl.ds(0, SUBS - 1)], coef_rsem.at[1])
         unpack(1)
-        drain(table_recv.at[pl.ds(0, HOMES - 1)], table_rsem.at[1])
+        drain(table_recv.at[pl.ds(0, 24)], pass_sem.at[1])
         plan(1, 1, me)
         fill(1, 1)
         reply(1, 1)
@@ -453,7 +472,8 @@
     def _():
         drain(coef_recv.at[pl.ds(0, 2 * SUBS - 1)], coef_ssem)
         drain(part_recv.at[0], part_ssem)
-        drain(table_recv.at[pl.ds(0, 2 * HOMES - 1)], table_ssem)
+        drain(table_recv.at[pl.ds(0, HOMES + 7)], table_ssem)
+        drain(table_recv.at[pl.ds(0, 24)], pass_sem.at[0])
         drain(client_v, client_sem.at[0])
         drain(reply_send.at[pl.ds(0, HOMES - 1)], reply_ssem)
 
@@ -521,6 +541,7 @@
         dma((2,)),
         dma((2,)),
         dma((2,)),
+        dma((2,)),
     ]
     return pl.pallas_call(
         kernel,

time: 24.5 us -> 22.8 us (0.931)
  Pallas kernels: 23.8 us -> 22.1 us
    pallas_call x1, Pallas kernels: 23.8 us -> 22.1 us  [shards(): pl.pallas_call(kernel, out_shape=jax.ShapeDtypeStruct(vectors.shape, BF16...]
where the time goes in v4:
time: 22.8 us
  Pallas kernels  22.1 us (97%)
  local copies, waits for them, and re-layouts  0.62 us (3%)
    pallas_call x1, Pallas kernels, shards(): pl.pallas_call(kernel, out_shape=jax.ShapeDtypeStruct(vectors.shape, BF16...  22.1 us
    unnamed x1, local copies, waits for them, and re-layouts  0.62 us

profile of v4, /device:TPU:1, one launch (start us, length us, event | category | flops | bytes accessed | tf_op | source)
XLA Modules:
  0.0 22.8 jit_solution(14180447819840321045)
XLA Ops:
  0.0 22.1 %product.1 = bf16[8,2048]{1,0:T(8,128)(2,1)S(1)} custom-call(bf16[8,2048]{1,0:T(8,128)(2,1)} %vec_hbm.1, bf16[8,64,256]{2,1,0:T(8,128)(2,1)} %basis_hbm.1, bf16[8,256,768]{2,1,0:T(8,128)(2,1)} %near_hbm.1, bf16[8,64,64]{2,1,0:T(8,128)(2,1)} %trans_hbm.1, s32[8,8]{1,0:T(8,128)} %tree_hbm.1, s32[8,8]{1,0:T(8,128)} %offset_hbm.1, ...), custom_call_target="tpu_custom_call" | custom-call | tf_op jit(solution)/shard_map/product/pallas_call | solution.py:546
  22.2 0.6 %copy.11 = bf16[8,2048]{1,0:T(8,128)(2,1)} copy(bf16[8,2048]{1,0:T(8,128)(2,1)S(1)} %product.1) | data formatting | bytes 65536

commit v5 on v4

--- a/solution.py
+++ b/solution.py
@@ -94,35 +94,6 @@
             device_id={"leaf": leaf, "sub": s}, device_id_type=MESH,
         ).start()
 
-    @pl.when(late == 0)
-    def _():
-        def greet_late(i, carry):
-            y, c = lax.rem(i, 8) // 2, lax.rem(i, 2)
-            announce(lax.rem(me // 16 + y, 4) * 16 + (7 - i // 8) * 2 + c, sub)
-            return carry
-
-        def greet(i, carry):
-            announce(home_leaf(lax.rem(j + i, HOMES)), sub)
-            return carry
-
-        for i in range(1, SUBS):
-            announce(other, lax.rem(sub + i, SUBS))
-        for leaf in (me, other):
-            for by in (-1, 1):
-                announce(*step(leaf, sub, by))
-        lax.fori_loop(0, HOMES, greet_late, 0, unroll=True)
-        lax.fori_loop(1, HOMES, greet, 0, unroll=True)
-
-    @pl.when(late == 1)
-    def _():
-        for i in range(1, 4):
-            announce(mirror(home_leaf(lax.rem(j + 8 * i, HOMES))), sub)
-        for i in range(1, 8):
-            announce(mirror(home_leaf(row + lax.rem(j + i, 8))), sub)
-
-    for i in range(1, SUBS):
-        announce(me, lax.rem(sub + i, SUBS))
-
     get_tree = pltpu.make_async_copy(tree_hbm, tree_v, sem_table.at[0])
     get_offset = pltpu.make_async_copy(offset_hbm, offset_v, sem_table.at[1])
     get_top = pltpu.make_async_copy(top_hbm, top_v, sem_table.at[2])
@@ -134,12 +105,92 @@
     get_near = [
         pltpu.make_async_copy(near_hbm.at[l], near_v.at[l], sem_near.at[l]) for l in range(LEAVES)
     ]
-    for copy in (get_tree, get_offset, get_top, get_x, get_basis, get_trans):
-        copy.start()
-    get_far.start()
-    get_root.start()
-    for copy in get_near:
-        copy.start()
+    now = (get_x, get_basis, get_trans, get_tree, get_offset, get_top)
+    soon = (get_far, get_root, *get_near)
+
+    @pl.when(late == 1)
+    def _():
+        for copy in now:
+            copy.start()
+
+    @pl.when(late == 0)
+    def _():
+        def greet_late(i, carry):
+            y, c = lax.rem(i, 8) // 2, lax.rem(i, 2)
+            announce(lax.rem(me // 16 + y, 4) * 16 + (7 - i // 8) * 2 + c, sub)
+            return carry
+
+        def greet(i, carry):
+            announce(home_leaf(lax.rem(j + i, HOMES)), sub)
+            return carry
+
+        lax.fori_loop(0, 16, greet_late, 0, unroll=True)
+        for i in range(1, SUBS):
+            announce(other, lax.rem(sub + i, SUBS))
+        for leaf in (me, other):
+            for by in (-1, 1):
+                announce(*step(leaf, sub, by))
+        lax.fori_loop(1, HOMES, greet, 0, unroll=True)
+        lax.fori_loop(16, HOMES, greet_late, 0, unroll=True)
+
+    @pl.when(late == 1)
+    def _():
+        for i in range(1, 4):
+            announce(mirror(home_leaf(lax.rem(j + 8 * i, HOMES))), sub)
+        for i in range(1, 8):
+            announce(mirror(home_leaf(row + lax.rem(j + i, 8))), sub)
+
+    for i in range(1, SUBS):
+        announce(me, lax.rem(sub + i, SUBS))
+
+    @pl.when(late == 0)
+    def _():
+        for copy in (*now, *soon):
+            copy.start()
+
+    get_x.wait()
+    get_basis.wait()
+    coefs = [
+        dot_nt(x_v[:, l * WIDTH : (l + 1) * WIDTH], basis_v[l]).astype(BF16) for l in range(LEAVES)
+    ]
+    for l in range(0, LEAVES, 2):
+        coef_send[l // 2] = jnp.concatenate(
+            [coefs[l].astype(F32), coefs[l + 1].astype(F32)], axis=1
+        ).astype(BF16)
+    get_trans.wait()
+    terms = [dot(coefs[l], trans_v[l]) for l in range(LEAVES)]
+    partial = functools.reduce(jnp.add, terms)
+    part_send[...] = jnp.concatenate([partial[0 : NVEC // 2], partial[NVEC // 2 :]], axis=1)
+
+    def send_part(leaf, s):
+        send(part_send, part_recv.at[late, sub], part_ssem, part_rsem.at[late], leaf, s)
+
+    def send_coefs(leaf, s):
+        send(coef_send, coef_recv.at[late * SUBS + sub], coef_ssem, coef_rsem.at[late], leaf, s)
+
+    @pl.when(late == 0)
+    def _():
+        pl.semaphore_wait(barrier, HOMES - 1 + SUBS - 1 + 2)
+        for i in range(1, SUBS):
+            send_part(me, lax.rem(sub + i, SUBS))
+        for i in range(1, SUBS):
+            send_coefs(me, lax.rem(sub + i, SUBS))
+        coef_recv[pl.ds(sub, 1)] = coef_send[...][None]
+        part_recv[0, pl.ds(sub, 1)] = part_send[...][None]
+
+    @pl.when(late == 1)
+    def _():
+        pl.semaphore_wait(barrier, HOMES + 7 + 3 + 2 * (SUBS - 1) + 2)
+        for i in range(SUBS):
+            send_part(other, lax.rem(sub + i, SUBS))
+        for i in range(SUBS):
+            send_coefs(other, lax.rem(sub + i, SUBS))
+        for i in range(1, SUBS):
+            send(
+                coef_send, coef_recv.at[SUBS + sub], coef_ssem, coef_rsem.at[1],
+                me, lax.rem(sub + i, SUBS),
+            )
+        coef_recv[pl.ds(SUBS + sub, 1)] = coef_send[...][None]
 
     get_tree.wait()
     get_offset.wait()
@@ -161,50 +212,6 @@
     table_row = table_row.astype(jnp.int32)
     table_send[...] = table_row
 
-    get_x.wait()
-    get_basis.wait()
-    coefs = [
-        dot_nt(x_v[:, l * WIDTH : (l + 1) * WIDTH], basis_v[l]).astype(BF16) for l in range(LEAVES)
-    ]
-    for l in range(0, LEAVES, 2):
-        coef_send[l // 2] = jnp.concatenate(
-            [coefs[l].astype(F32), coefs[l + 1].astype(F32)], axis=1
-        ).astype(BF16)
-    get_trans.wait()
-    terms = [dot(coefs[l], trans_v[l]) for l in range(LEAVES)]
-    partial = functools.reduce(jnp.add, terms)
-    part_send[...] = jnp.concatenate([partial[0 : NVEC // 2], partial[NVEC // 2 :]], axis=1)
-
-    def send_part(leaf, s):
-        send(part_send, part_recv.at[late, sub], part_ssem, part_rsem.at[late], leaf, s)
-
-    def send_coefs(leaf, s):
-        send(coef_send, coef_recv.at[late * SUBS + sub], coef_ssem, coef_rsem.at[late], leaf, s)
-
-    @pl.when(late == 0)
-    def _():
-        pl.semaphore_wait(barrier, HOMES - 1 + SUBS - 1 + 2)
-        for i in range(1, SUBS):
-            send_part(me, lax.rem(sub + i, SUBS))
-        for i in range(1, SUBS):
-            send_coefs(me, lax.rem(sub + i, SUBS))
-        coef_recv[pl.ds(sub, 1)] = coef_send[...][None]
-        part_recv[0, pl.ds(sub, 1)] = part_send[...][None]
-
-    @pl.when(late == 1)
-    def _():
-        pl.semaphore_wait(barrier, HOMES + 7 + 3 + 2 * (SUBS - 1) + 2)
-        for i in range(SUBS):
-            send_part(other, lax.rem(sub + i, SUBS))
-        for i in range(SUBS):
-            send_coefs(other, lax.rem(sub + i, SUBS))
-        for i in range(1, SUBS):
-            send(
-                coef_send, coef_recv.at[SUBS + sub], coef_ssem, coef_rsem.at[1],
-                me, lax.rem(sub + i, SUBS),
-            )
-        coef_recv[pl.ds(SUBS + sub, 1)] = coef_send[...][None]
-
     @pl.when(late == 0)
     def _():
         table_recv[pl.ds(j, 1)] = table_send[...][None]
@@ -237,6 +244,11 @@
             vec_hbm.at[:, pl.ds(start, WIDTH)], halo_v.at[kind, side],
             halo_ssem, halo_rsem.at[kind, side], leaf, s,
         )
+
+    @pl.when(late == 1)
+    def _():
+        for copy in soon:
+            copy.start()
 
     entry = iota((64, LINKS), 0)
     link = iota((64, LINKS), 1)

time: 22.8 us -> 22.7 us (level)
  no operation moved by 1% of the time
where the time goes in v5:
time: 22.7 us; the launch traced here: 22.6 us
  Pallas kernels  22 us (97%)
  local copies, waits for them, and re-layouts  0.62 us (3%)
    pallas_call x1, Pallas kernels, shards(): pl.pallas_call(kernel, out_shape=jax.ShapeDtypeStruct(vectors.shape, BF16...  22 us
    unnamed x1, local copies, waits for them, and re-layouts  0.62 us

profile of v5, /device:TPU:1, one launch (start us, length us, event | category | flops | bytes accessed | tf_op | source)
XLA Modules:
  0.0 22.6 jit_solution(10808597455272853605)
XLA Ops:
  0.0 22.0 %product.1 = bf16[8,2048]{1,0:T(8,128)(2,1)S(1)} custom-call(bf16[8,2048]{1,0:T(8,128)(2,1)} %vec_hbm.1, bf16[8,64,256]{2,1,0:T(8,128)(2,1)} %basis_hbm.1, bf16[8,256,768]{2,1,0:T(8,128)(2,1)} %near_hbm.1, bf16[8,64,64]{2,1,0:T(8,128)(2,1)} %trans_hbm.1, s32[8,8]{1,0:T(8,128)} %tree_hbm.1, s32[8,8]{1,0:T(8,128)} %offset_hbm.1, ...), custom_call_target="tpu_custom_call" | custom-call | tf_op jit(solution)/shard_map/product/pallas_call | solution.py:558
  22.0 0.6 %copy.11 = bf16[8,2048]{1,0:T(8,128)(2,1)} copy(bf16[8,2048]{1,0:T(8,128)(2,1)S(1)} %product.1) | data formatting | bytes 65536

commit v6 on v4

--- a/solution.py
+++ b/solution.py
@@ -60,7 +60,7 @@
     slot_s, top_slot_s, client_s,
     table_send, table_recv, coef_send, coef_recv, part_send, part_recv, wide_v, both_v, plan_v,
     node_send, node_recv, node_mine, node_theirs, halo_v,
-    reply_send, reply_recv, picked_v, rank_v, pairs_v, down_v, local_v,
+    reply_send, reply_recv, picked_v, rank_v, pairs_v, root_pairs_v, down_v, local_v,
     sem_x, sem_basis, sem_near, sem_trans, sem_table, sem_far, sem_root, sem_smem,
     halo_ssem, halo_rsem, table_ssem, table_rsem, coef_ssem, coef_rsem, part_ssem, part_rsem,
     node_ssem, node_rsem, reply_ssem, reply_rsem, fwd_sem, pick_sem, client_sem, pass_sem,
@@ -110,8 +110,9 @@
         for leaf in (me, other):
             for by in (-1, 1):
                 announce(*step(leaf, sub, by))
-        lax.fori_loop(0, HOMES, greet_late, 0, unroll=True)
+        lax.fori_loop(0, 16, greet_late, 0, unroll=True)
         lax.fori_loop(1, HOMES, greet, 0, unroll=True)
+        lax.fori_loop(16, HOMES, greet_late, 0, unroll=True)
 
     @pl.when(late == 1)
     def _():
@@ -257,6 +258,12 @@
                 [far_v[l, f], far_v[l, f + 1]], axis=1
             )
 
+    get_root.wait()
+    for f in range(0, LINKS, 2):
+        root_pairs_v[:, f * RANK : (f + 2) * RANK] = jnp.concatenate(
+            [root_v[0, f], root_v[0, f + 1]], axis=1
+        )
+
     def near(l, before, after):
         middle = x_v[:, l * WIDTH : (l + 1) * WIDTH]
         span = jnp.concatenate([before, middle, after], axis=1)
@@ -267,7 +274,6 @@
         near(l, x_v[:, (l - 1) * WIDTH : l * WIDTH], x_v[:, (l + 1) * WIDTH : (l + 2) * WIDTH])
     get_near[0].wait()
     get_near[LEAVES - 1].wait()
-    get_root.wait()
     get_slot.wait()
     get_top_slot.wait()
 
@@ -384,6 +390,7 @@
         drain(client_v, client_sem.at[1])
         get_client = pltpu.make_async_copy(client_v, client_s, sem_smem.at[0])
         get_client.start()
+        get_client.wait()
         plan(0, 1, me)
         fill(0, 1)
         reply(0, 1)
@@ -392,11 +399,7 @@
                 drain(halo_v.at[kind, side], halo_rsem.at[kind, side])
         send(halo_v.at[1], halo_v.at[0], fwd_sem.at[0], fwd_sem.at[1], other, sub)
         near_ends()
-        get_client.wait()
         drain(node_recv.at[pl.ds(0, 2 * HOMES - 2)], node_rsem)
-        for f in range(LINKS):
-            node_theirs[f] = node_recv[client_s[0, f]]
-        send(node_theirs, node_mine, pick_sem.at[0], pick_sem.at[1], other, sub)
         for f in range(LINKS):
             node_mine[f] = node_recv[top_slot_s[0, f]]
 
@@ -412,12 +415,14 @@
         near_ends()
         drain(node_mine, pick_sem.at[1])
 
-    terms = []
-    for f in range(LINKS):
-        n = node_mine[f].astype(F32)
-        n = jnp.concatenate([n[:, 0:64], n[:, 64:128]], axis=0).astype(BF16)
-        terms.append(dot_nt(n, root_v[0, f]))
-    root_local = functools.reduce(jnp.add, terms)
+    left = iota((NVEC // 2, 128), 1) < 64
+    parts = []
+    for f in range(0, LINKS, 2):
+        even, odd = node_mine[f].astype(F32), node_mine[f + 1].astype(F32)
+        top = jnp.where(left, even, pltpu.roll(odd, 64, 1))
+        bottom = jnp.where(left, pltpu.roll(even, 64, 1), odd)
+        parts.append(jnp.concatenate([top, bottom], axis=0))
+    root_local = dot_nt(jnp.concatenate(parts, axis=1).astype(BF16), root_pairs_v[...])
     hi = root_local.astype(BF16)
     rest = root_local - hi.astype(F32)
     mid = rest.astype(BF16)
@@ -430,6 +435,9 @@
 
     @pl.when(late == 0)
     def _():
+        for f in range(LINKS):
+            node_theirs[f] = node_recv[client_s[0, f]]
+        send(node_theirs, node_mine, pick_sem.at[0], pick_sem.at[1], other, sub)
         drain(reply_recv.at[pl.ds(0, 2 * HOMES - 2)], reply_rsem)
 
     @pl.when(late == 1)
@@ -516,6 +524,7 @@
         pltpu.VMEM((4, HOMES, NVEC, 128), F32),
         pltpu.VMEM((64, 128), F32),
         pltpu.VMEM((LEAVES, RANK, LINKS * RANK), BF16),
+        pltpu.VMEM((RANK, LINKS * RANK), BF16),
         pltpu.VMEM((LEAVES, NVEC, RANK), F32),
         pltpu.VMEM((NVEC, LEAVES * WIDTH), F32),
         dma,

time: 22.8 us -> 22.9 us (level)
  no operation moved by 1% of the time
where the time goes in v6:
time: 22.9 us; the launch traced here: 22.8 us
  Pallas kernels  22.2 us (97%)
  local copies, waits for them, and re-layouts  0.62 us (3%)
    pallas_call x1, Pallas kernels, shards(): pl.pallas_call(kernel, out_shape=jax.ShapeDtypeStruct(vectors.shape, BF16...  22.2 us
    unnamed x1, local copies, waits for them, and re-layouts  0.62 us

profile of v6, /device:TPU:1, one launch (start us, length us, event | category | flops | bytes accessed | tf_op | source)
XLA Modules:
  0.0 22.8 jit_solution(10111655759534641258)
XLA Ops:
  0.0 22.2 %product.1 = bf16[8,2048]{1,0:T(8,128)(2,1)S(1)} custom-call(bf16[8,2048]{1,0:T(8,128)(2,1)} %vec_hbm.1, bf16[8,64,256]{2,1,0:T(8,128)(2,1)} %basis_hbm.1, bf16[8,256,768]{2,1,0:T(8,128)(2,1)} %near_hbm.1, bf16[8,64,64]{2,1,0:T(8,128)(2,1)} %trans_hbm.1, s32[8,8]{1,0:T(8,128)} %tree_hbm.1, s32[8,8]{1,0:T(8,128)} %offset_hbm.1, ...), custom_call_target="tpu_custom_call" | custom-call | tf_op jit(solution)/shard_map/product/pallas_call | solution.py:555
  22.2 0.6 %copy.11 = bf16[8,2048]{1,0:T(8,128)(2,1)} copy(bf16[8,2048]{1,0:T(8,128)(2,1)S(1)} %product.1) | data formatting | bytes 65536
